TPU v7x, 512 devices: a whole 4x4x16 slice. The times are simulated.
512 devices in a mesh: wrk: 32 (over x, y, core), emp: 16 (over z).
Axes of the slice: x: 4, y: 4, z: 16, core: 2. Of those that a mesh axis runs over, the one named last changes fastest.
Arguments:
- worker_emb: bfloat16 [524288, 256], P(('wrk', 'emp')), may hold values from -6 to 6
- employer_emb: bfloat16 [256, 131072], P('wrk', 'emp'), may hold values from -6 to 6
- eligible: int32 [512, 512], P('wrk', 'emp'), may hold values from 0 to 1, as said below
- worker_mass: float32 [524288], P('wrk'), may hold values from 0.5 to 2
- employer_mass: float32 [131072], P('emp'), may hold values from 0.5 to 2
Outputs:
- worker_potential: float32 [524288], P('wrk')
- employer_potential: float32 [131072], P('emp')
Inputs may be any that keep to these rules, and one draw needn't show every extreme that they name: eligible holds 0 or 1. The 16 x 32 sub-block of one device (block rows of one index of wrk, block columns of one index of emp) holds at most 12 ones, and some device holds exactly 12. Every block row and every block column holds at least one one.
All inputs are finite; a program needn't handle non-finite values.
Results may differ from a plain program's by a relative error of at most 0.0003.
Values may be sent and summed in bfloat16 or wider, within the bound.
A program may use at most 64 MiB of HBM per device.

v0:
```python
import jax
import jax.numpy as jnp
from jax import lax
from jax.sharding import PartitionSpec as P

E = 256
CAP = 12
ITERS = 3


SOFTMAX_TEMP = 0.25
EPSILON = 1e-06
highest = lax.Precision.HIGHEST


def shards(worker_emb, employer_emb, eligible, worker_mass, employer_mass):
    worker_rows = lax.all_gather(worker_emb, "emp", axis=0, tiled=True)
    employer_cols = lax.all_gather(employer_emb, "wrk", axis=0, tiled=True)
    row_blocks = eligible.shape[0]
    col_blocks = eligible.shape[1]
    block_rows = worker_rows.shape[0] // row_blocks
    block_cols = employer_cols.shape[1] // col_blocks
    inv_worker = lax.rsqrt(jnp.mean(jnp.square(worker_rows.astype(jnp.float32)), axis=1) + EPSILON)
    inv_employer = lax.rsqrt(
        jnp.mean(jnp.square(employer_cols.astype(jnp.float32)), axis=0) + EPSILON
    )
    flat = eligible.reshape(-1)
    slot_order = jnp.argsort(1 - flat, stable=True)[:CAP]
    usable = flat[slot_order].astype(jnp.float32)
    row_index = slot_order // col_blocks
    col_index = slot_order % col_blocks
    row_onehot = (row_index[:, None] == jnp.arange(row_blocks, dtype=jnp.int32)[None, :]).astype(
        jnp.float32
    )
    col_onehot = (col_index[:, None] == jnp.arange(col_blocks, dtype=jnp.int32)[None, :]).astype(
        jnp.float32
    )

    def make_tile(row_pick, col_pick, keep_mask):
        row_slab = lax.dynamic_slice_in_dim(worker_rows, row_pick * block_rows, block_rows, 0)
        col_slab = lax.dynamic_slice_in_dim(employer_cols, col_pick * block_cols, block_cols, 1)
        row_scale = lax.dynamic_slice_in_dim(inv_worker, row_pick * block_rows, block_rows, 0)
        col_scale = lax.dynamic_slice_in_dim(inv_employer, col_pick * block_cols, block_cols, 0)
        cosine_similarity = jnp.dot(row_slab, col_slab, preferred_element_type=jnp.float32)
        cosine_similarity = cosine_similarity * row_scale[:, None] * col_scale[None, :] / E
        return (jnp.exp((cosine_similarity - 1.0) / SOFTMAX_TEMP) * keep_mask).astype(jnp.bfloat16)

    stacked = lax.map(
        lambda packed: make_tile(packed[0], packed[1], packed[2]), (row_index, col_index, usable)
    )
    source = (stacked,)

    def fetch(packed):
        return packed[0]

    def row_product(packed):
        return jnp.dot(fetch(packed).astype(jnp.float32), packed[-1], precision=highest)

    def col_product(packed):
        return jnp.dot(packed[-1], fetch(packed).astype(jnp.float32), precision=highest)

    employer_scaling = jnp.ones((col_blocks * block_cols,), jnp.float32)
    worker_scaling = jnp.ones((row_blocks * block_rows,), jnp.float32)
    for step in range(ITERS):
        col_vectors = jnp.dot(
            col_onehot, employer_scaling.reshape(col_blocks, block_cols), precision=highest
        )
        row_part = lax.map(row_product, source + (col_vectors,))
        row_local = jnp.dot(row_onehot.T, row_part, precision=highest).reshape(-1)
        row_total = lax.psum(row_local, "emp")
        worker_scaling = worker_mass / row_total
        row_embedding_vectors = jnp.dot(
            row_onehot, worker_scaling.reshape(row_blocks, block_rows), precision=highest
        )
        col_part = lax.map(col_product, source + (row_embedding_vectors,))
        col_local = jnp.dot(col_onehot.T, col_part, precision=highest).reshape(-1)
        column_total = lax.psum(col_local, "wrk")
        employer_scaling = employer_mass / column_total
    return (SOFTMAX_TEMP * jnp.log(worker_scaling), SOFTMAX_TEMP * jnp.log(employer_scaling))


def solution(mesh):
    return jax.shard_map(
        shards,
        mesh=mesh,
        in_specs=(P(("wrk", "emp"), None), P("wrk", "emp"), P("wrk", "emp"), P("wrk"), P("emp")),
        out_specs=(P("wrk"), P("emp")),
        check_vma=False,
    )
```

profile of v0, /device:TPU:1, one launch (start us, length us, event | category | flops | bytes accessed | tf_op | source)
XLA Modules:
  0.0 1137.5 jit_solution(2567897181313042351)
XLA Ops:
  9.5 3.8 sort.17
  14.1 64.1 %all-gather.5.cloned.1.call-done = bf16[256,8192]{1,0:T(8,128)(2,1)} async-done(((bf16[8,8192]{1,0:T(8,128)(2,1)}), bf16[256,8192]{1,0:T(8,128)(2,1)}) %all-gather.5.cloned.1.call-update) | async-done | bytes 4194320 | tf_op jit(solution)/shard_map/all_gather | solution.py:18
  78.3 3.1 multiply_reduce_fusion.1
  81.4 104.0 %all-gather.3.cloned.1.call-done = bf16[16384,256]{1,0:T(8,128)(2,1)} async-done(((bf16[1024,256]{1,0:T(8,128)(2,1)}), bf16[16384,256]{1,0:T(8,128)(2,1)}) %all-gather.3.cloned.1.call-update) | async-done | bytes 8388624 | tf_op jit(solution)/shard_map/all_gather | solution.py:17
  185.4 5.2 multiply_reduce_fusion
  190.7 74.0 %while.72 = (s32[]{:T(128)}, bf16[12,1024,256]{2,1,0:T(8,128)(2,1)}, s32[12]{0:T(128)S(1)}, bf16[16384,256]{1,0:T(8,128)(2,1)}, s32[12]{0:T(128)S(1)}, /*index=5...) while((s32[]{:T(128)}, ...), condition=%wide.region_4.5_spmd, body=%wide.region_3.4_spmd.sunk | while | flops 136052752 | bytes 1196317 | solution.py:48
  193.8 3.0 fusion.102
  200.0 3.1 fusion.102
  206.2 3.0 fusion.102
  212.4 3.0 fusion.102
  218.5 3.0 fusion.102
  224.7 3.0 fusion.102
  230.9 3.0 fusion.102
  237.0 3.0 fusion.102
  243.2 3.0 fusion.102
  249.3 3.0 fusion.102
  255.5 3.0 fusion.102
  261.6 3.0 fusion.102
  264.6 19.9 %while.73 = (s32[]{:T(128)}, f32[12,1024]{1,0:T(8,128)S(1)}, bf16[12,1024,256]{2,1,0:T(8,128)(2,1)}, f32[12,256]{1,0:T(8,128)S(1)}, s32[]{:T(128)}, /*index=5*/s32[]{:T(128)}) while((s32[]{:T(128)}, f32[12,1024]{1,0:T(8,128)S(1)}, bf16[12,1024,256]{2,1,0:T(8,128)(2,1)}, f32[12,256]{1,0:T(8,128)S(1)}, s32[]{:T(128)}, ...), condition=%wide.region_6.7_spmd, body=%wide.region_5.6_spmd.sunk | while | flops 3145730 | bytes 538697 | solution.py:68
  264.6 1.5 fusion.105
  269.6 1.5 fusion.105
  285.6 120.5 %all-reduce.4.cloned.1.call-done = f32[16384]{0:T(1024)} async-done(((f32[16384]{0:T(1024)}), f32[16384]{0:T(1024)}) %all-reduce.4.cloned.1.call-update) | async-done | bytes 65552 | tf_op jit(solution)/shard_map/psum | solution.py:70
  407.2 16.9 %while.74 = (s32[]{:T(128)}, f32[12,256]{1,0:T(8,128)S(1)}, f32[12,1024]{1,0:T(8,128)S(1)}, bf16[12,1024,256]{2,1,0:T(8,128)(2,1)}, s32[]{:T(128)}, /*index=5*/s32[]{:T(128)}) while((s32[]{:T(128)}, f32[12,256]{1,0:T(8,128)S(1)}, f32[12,1024]{1,0:T(8,128)S(1)}, bf16[12,1024,256]{2,1,0:T(8,128)(2,1)}, s32[]{:T(128)}, ...), condition=%wide.region_9.10_spmd, body=%wide.region_8.9_spmd.sunk | while | flops 3145730 | bytes 532553 | solution.py:75
  424.4 129.8 %psum.43 = f32[8192]{0:T(1024)S(1)} all-reduce(f32[8192]{0:T(1024)S(1)} %bitcast.119), channel_id=1, replica_groups=mesh['wrk'=32,'emp'=16] {'wrk'}, use_global_device_ids=true, to_apply=%region_10.11 | all-reduce | flops 8192 | bytes 65536 | tf_op jit(solution)/shard_map/psum | solution.py:77
  554.5 19.9 %while.75 = (s32[]{:T(128)}, f32[12,1024]{1,0:T(8,128)S(1)}, bf16[12,1024,256]{2,1,0:T(8,128)(2,1)}, f32[12,256]{1,0:T(8,128)S(1)}, s32[]{:T(128)}, /*index=5*/s32[]{:T(128)}) while((s32[]{:T(128)}, f32[12,1024]{1,0:T(8,128)S(1)}, bf16[12,1024,256]{2,1,0:T(8,128)(2,1)}, f32[12,256]{1,0:T(8,128)S(1)}, s32[]{:T(128)}, ...), condition=%wide.region_12.13_spmd, body=%wide.region_11.12_spmd.sunk | while | flops 3145730 | bytes 538697 | solution.py:68
  575.5 118.4 %all-reduce.6.cloned.1.call-done = f32[16384]{0:T(1024)} async-done(((f32[16384]{0:T(1024)}), f32[16384]{0:T(1024)}) %all-reduce.6.cloned.1.call-update) | async-done | bytes 65552 | tf_op jit(solution)/shard_map/psum | solution.py:70
  694.9 16.9 %while.76 = (s32[]{:T(128)}, f32[12,256]{1,0:T(8,128)S(1)}, f32[12,1024]{1,0:T(8,128)S(1)}, bf16[12,1024,256]{2,1,0:T(8,128)(2,1)}, s32[]{:T(128)}, /*index=5*/s32[]{:T(128)}) while((s32[]{:T(128)}, f32[12,256]{1,0:T(8,128)S(1)}, f32[12,1024]{1,0:T(8,128)S(1)}, bf16[12,1024,256]{2,1,0:T(8,128)(2,1)}, s32[]{:T(128)}, ...), condition=%wide.region_15.16_spmd, body=%wide.region_14.15_spmd.sunk | while | flops 3145730 | bytes 532553 | solution.py:75
  712.1 129.8 %psum.45 = f32[8192]{0:T(1024)S(1)} all-reduce(f32[8192]{0:T(1024)S(1)} %bitcast.120), channel_id=1, replica_groups=mesh['wrk'=32,'emp'=16] {'wrk'}, use_global_device_ids=true, to_apply=%region_16.17 | all-reduce | flops 8192 | bytes 65536 | tf_op jit(solution)/shard_map/psum | solution.py:77
  842.2 19.9 %while.77 = (s32[]{:T(128)}, f32[12,1024]{1,0:T(8,128)S(1)}, bf16[12,1024,256]{2,1,0:T(8,128)(2,1)}, f32[12,256]{1,0:T(8,128)S(1)}, s32[]{:T(128)}, /*index=5*/s32[]{:T(128)}) while((s32[]{:T(128)}, f32[12,1024]{1,0:T(8,128)S(1)}, bf16[12,1024,256]{2,1,0:T(8,128)(2,1)}, f32[12,256]{1,0:T(8,128)S(1)}, s32[]{:T(128)}, ...), condition=%wide.region_18.19_spmd, body=%wide.region_17.18_spmd.sunk | while | flops 3145730 | bytes 538697 | solution.py:68
  863.1 118.4 %all-reduce.8.cloned.1.call-done = f32[16384]{0:T(1024)} async-done(((f32[16384]{0:T(1024)}), f32[16384]{0:T(1024)}) %all-reduce.8.cloned.1.call-update) | async-done | bytes 65552 | tf_op jit(solution)/shard_map/psum | solution.py:70
  983.3 16.9 %while.78 = (s32[]{:T(128)}, f32[12,256]{1,0:T(8,128)S(1)}, f32[12,1024]{1,0:T(8,128)S(1)}, bf16[12,1024,256]{2,1,0:T(8,128)(2,1)}, s32[]{:T(128)}, /*index=5*/s32[]{:T(128)}) while((s32[]{:T(128)}, f32[12,256]{1,0:T(8,128)S(1)}, f32[12,1024]{1,0:T(8,128)S(1)}, bf16[12,1024,256]{2,1,0:T(8,128)(2,1)}, s32[]{:T(128)}, ...), condition=%wide.region_21.22_spmd, body=%wide.region_20.21_spmd.sunk | while | flops 3145730 | bytes 532553 | solution.py:75
  1000.5 129.8 %psum.47 = f32[8192]{0:T(1024)S(1)} all-reduce(f32[8192]{0:T(1024)S(1)} %bitcast.121), channel_id=1, replica_groups=mesh['wrk'=32,'emp'=16] {'wrk'}, use_global_device_ids=true, to_apply=%region_22.23 | all-reduce | flops 8192 | bytes 65536 | tf_op jit(solution)/shard_map/psum | solution.py:77
  (262 shorter events, 139.9 us)
Async XLA Ops:
  7.2 71.1 %all-gather.5.cloned.1.call-start = ((), (), s32[]{:S(2)}) async-start(), calls=%async_computation.1 | async-start | bytes 4325376 | tf_op jit(solution)/shard_map/all_gather | solution.py:18
  7.9 177.5 %all-gather.3.cloned.1.call-start = ((), (), s32[]{:S(2)}) async-start(), calls=%async_computation | async-start | bytes 8912896 | tf_op jit(solution)/shard_map/all_gather | solution.py:17
  8.6 397.4 %all-reduce.4.cloned.1.call-start = ((), (), s32[]{:S(2)}) async-start(), calls=%async_computation.2 | async-start | bytes 131072 | tf_op jit(solution)/shard_map/psum | solution.py:70
  190.7 215.4 %copy-start = (f32[16384]{0:T(1024)S(1)}, f32[16384]{0:T(1024)}, u32[]{:S(2)}) copy-start(f32[16384]{0:T(1024)} %param.22) | copy-start | bytes 196612
  264.6 289.6 %copy-start.1 = (f32[8192]{0:T(1024)S(1)}, f32[8192]{0:T(1024)}, u32[]{:S(2)}) copy-start(f32[8192]{0:T(1024)} %param.23) | copy-start | bytes 98308
  285.6 408.3 %all-reduce.6.cloned.1.call-start = ((), (), s32[]{:S(2)}) async-start(), calls=%async_computation.3 | async-start | bytes 131072 | tf_op jit(solution)/shard_map/psum | solution.py:70
  575.4 406.1 %all-reduce.8.cloned.1.call-start = ((), (), s32[]{:S(2)}) async-start(), calls=%async_computation.4 | async-start | bytes 131072 | tf_op jit(solution)/shard_map/psum | solution.py:70
Sparse Core Ops, SparseCore 0:
  11.1 67.1 all-gather.4
  80.4 104.9 all-gather.2
  285.7 120.3 all-reduce.3
  575.5 118.2 all-reduce.5
  863.2 118.2 all-reduce.7
where the time goes:
time: 1140 us
  waiting for transfers between devices  527 us (46%)
  blocking collectives  389 us (34%)
  matrix products  144 us (13%)
  local copies, waits for them, and re-layouts  29.9 us (3%)
  loops' own time  17.5 us (2%)
  other arithmetic  16 us (1%)
  between operations  14.1 us (1%)
    psum x3, blocking collectives, shards(): column_total = lax.psum(col_local, 'wrk')  389 us
    psum x3, waiting for transfers between devices, shards(): row_total = lax.psum(row_local, 'emp')  357 us
    all_gather x1, waiting for transfers between devices, shards(): worker_rows = lax.all_gather(worker_emb, 'emp', axis=0, tiled=True)  104 us
    all_gather x1, waiting for transfers between devices, shards(): employer_cols = lax.all_gather(employer_emb, 'wrk', axis=0, tiled=True)  64.1 us
    dot_general x36, matrix products, row_product(): jnp.dot(fetch(packed).astype(jnp.float32), packed[-1], precision=highest)  55.8 us
    dot_general x36, matrix products, col_product(): jnp.dot(packed[-1], fetch(packed).astype(jnp.float32), precision=highest)  48.9 us
    dot_general x12, matrix products, make_tile(): jnp.dot(row_slab, col_slab, preferred_element_type=jnp.float32)  36 us
  transfers between devices with their start and end apart: 5, of which 5 were waited for; matrix products, arithmetic and copies ran while one was open for 1% of the time, Pallas kernels for 0%

commit v1 on v0

v1 whole, which is shorter than its diff:
```python
import functools

import jax
import jax.numpy as jnp
from jax import lax
from jax.experimental import pallas as pl
from jax.experimental.pallas import tpu as pltpu
from jax.sharding import PartitionSpec as P

E = 256
ITERS = 3
SOFTMAX_TEMP = 0.25
EPSILON = 1e-06
RW = 1024
RE = 256
SLOTS = (16, 48)
CHUNKS = 4
MESH = pl.DeviceIdType.MESH
VMEM = pl.BlockSpec(memory_space=pltpu.VMEM)
SMEM = pl.BlockSpec(memory_space=pltpu.SMEM)
ANY = pl.BlockSpec(memory_space=pl.ANY)
DMA = pltpu.SemaphoreType.DMA


def place():
    w, z = lax.axis_index("wrk"), lax.axis_index("emp")
    return w // 8, lax.rem(w // 2, 4), lax.rem(w, 2), z // 4, lax.rem(z, 4)


def device(x, y, c, z):
    return ((lax.rem(x, 4) * 4 + lax.rem(y, 4)) * 2 + c, lax.rem(z, 16))


def remote(src, dst, send, recv, to):
    return pltpu.make_async_remote_copy(
        src_ref=src, dst_ref=dst, send_sem=send, recv_sem=recv, device_id=to, device_id_type=MESH
    )


def took(ref, sem):
    pltpu.make_async_copy(ref, ref, sem).wait()


def gather_kernel(
    wk, em, small,
    rows, cols, small_out, peak_out,
    small_all, top, top_z, top_w,
    keep_sem, z_send, z_recv, xy_send, xy_recv, core_send, core_recv,
    row_send, row_recv, small_send, small_recv, top_send, top_recv,
):
    x, y, c, a, b = place()
    w, z = lax.axis_index("wrk"), lax.axis_index("emp")
    left, right = device(x + 3, y, c, z), device(x + 1, y, c, z)
    down, up = device(x, y + 3, c, z), device(x, y + 1, c, z)
    back, ahead = (w, lax.rem(z + 12, 16)), (w, lax.rem(z + 4, 16))
    twin = (w + 1 - 2 * c, z)

    barrier = pltpu.get_barrier_semaphore()

    def greet_z(d, _):
        pl.semaphore_signal(barrier, inc=1, device_id=(w, lax.rem(z + d, 16)), device_id_type=MESH)
        return 0

    def greet_w(d, _):
        pl.semaphore_signal(barrier, inc=1, device_id=(lax.rem(w + d, 32), z), device_id_type=MESH)
        return 0

    lax.fori_loop(1, 16, greet_z, 0)
    lax.fori_loop(1, 32, greet_w, 0)
    keep = [
        pltpu.make_async_copy(em, cols.at[a, w], keep_sem.at[0]),
        pltpu.make_async_copy(wk, rows.at[b], keep_sem.at[1]),
    ]
    for one in keep:
        one.start()
    small_all[a] = small[...]
    pl.semaphore_wait(barrier, 46)

    remote(em, cols.at[a, w], z_send, z_recv.at[0], ahead).start()
    remote(em, cols.at[a, w], z_send, z_recv.at[1], back).start()
    for d in (1, 2, 3):
        remote(
            small, small_all.at[a], small_send, small_recv, (w, lax.rem(z + 4 * d, 16))
        ).start()

    def unit(p, i, j):
        return cols.at[p, (lax.rem(x + i, 4) * 4 + lax.rem(y + j, 4)) * 2 + c]

    def half(ref, k):
        return ref.at[:, :, pl.ds(1024 * k, 1024)]

    def send_own(s, src):
        p = lax.rem(a + s, 4)
        for k, to in enumerate((right, left, up, down)):
            remote(src, cols.at[p, w], xy_send.at[k], xy_recv.at[s, k], to).start()
        remote(src, cols.at[p, w], core_send, core_recv, twin).start()

    def push(src, k, sem):
        to = (right, left, up, down)[k]
        remote(src, src, xy_send.at[k], sem, to).start()

    def relay_first(s):
        p = lax.rem(a + s, 4)
        for k, (i, j) in enumerate(((3, 0), (1, 0), (0, 3), (0, 1))):
            got = unit(p, i, j)
            took(got, xy_recv.at[s, k])
            push(half(got, k % 2), k, xy_recv.at[s, 4 + k // 2])
            if k < 2:
                push(got.at[0], 2, xy_recv.at[s, 6 + k])
                push(got.at[0], 3, xy_recv.at[s, 9 + k])
            else:
                push(got.at[1], 0, xy_recv.at[s, 12 + k - 2])
                push(got.at[1], 1, xy_recv.at[s, 15 + k - 2])

    def core_push(p, i, j):
        got = unit(p, i, j)
        remote(got, got, core_send, core_recv, twin).start()

    def relay_second(s):
        p = lax.rem(a + s, 4)
        got = unit(p, 2, 0)
        took(got, xy_recv.at[s, 4])
        push(got.at[0], 2, xy_recv.at[s, 8])
        push(got.at[0], 3, xy_recv.at[s, 11])
        got = unit(p, 0, 2)
        took(got, xy_recv.at[s, 5])
        push(got.at[1], 0, xy_recv.at[s, 14])
        push(got.at[1], 1, xy_recv.at[s, 17])
        for i, j in ((3, 0), (1, 0), (0, 3), (0, 1), (2, 0), (0, 2)):
            core_push(p, i, j)

    def relay_third(s, ms):
        p = lax.rem(a + s, 4)
        for m in ms:
            o = (3, 1, 2)[m]
            for k, (g, i, j) in enumerate(((0, o, 3), (0, o, 1), (1, 3, o), (1, 1, o))):
                got = unit(p, i, j).at[g]
                took(got, xy_recv.at[s, 6 + 3 * k + m])
                part = got.at[:, pl.ds(1024 * (k % 2), 1024)]
                push(part, (2, 3, 0, 1)[k], xy_recv.at[s, 18])

    def finish(s):
        p = lax.rem(a + s, 4)
        took(cols.at[p, pl.ds(0, 3)], xy_recv.at[s, 18])
        for i in (1, 2, 3):
            for j in (1, 2, 3):
                core_push(p, i, j)

    def row_chunk(block, j):
        return block.at[pl.ds(j * (RW // CHUNKS), RW // CHUNKS)]

    def send_rows():
        for j in range(CHUNKS):
            src = row_chunk(wk, j)

            @pl.when(b < 3)
            def _():
                remote(src, row_chunk(rows.at[b], j), row_send.at[0, 0], row_recv.at[0, 0, j], (w, z + 1)).start()

            @pl.when(b > 0)
            def _():
                remote(src, row_chunk(rows.at[b], j), row_send.at[1, 0], row_recv.at[1, 0, j], (w, z - 1)).start()

    def relay_rows(d):
        for j in range(CHUNKS):

            @pl.when(b >= d)
            def _():
                took(row_chunk(rows.at[b - d], j), row_recv.at[0, d - 1, j])

            if d < 3:

                @pl.when((b >= d) & (b < 3))
                def _():
                    got = row_chunk(rows.at[b - d], j)
                    remote(got, got, row_send.at[0, d], row_recv.at[0, d, j], (w, z + 1)).start()

            @pl.when(b + d <= 3)
            def _():
                took(row_chunk(rows.at[b + d], j), row_recv.at[1, d - 1, j])

            if d < 3:

                @pl.when((b + d <= 3) & (b > 0))
                def _():
                    got = row_chunk(rows.at[b + d], j)
                    remote(got, got, row_send.at[1, d], row_recv.at[1, d, j], (w, z - 1)).start()

    send_own(0, em)
    relay_first(0)
    relay_second(0)
    send_rows()
    relay_third(0, (0, 1))

    took(small_all.at[pl.ds(0, 3)], small_recv)
    flags = small_all[...]
    line = lax.broadcasted_iota(jnp.int32, flags.shape, 1)
    mine = (line >= 8 + 4 * a) & (line < 12 + 4 * a)
    top[0] = jnp.full((8, 128), jnp.sum(jnp.where(mine, flags, 0.0)), jnp.float32)

    def top_to_z(d, _):
        remote(top.at[0], top_z.at[d - 1], top_send.at[0], top_recv.at[0], (w, lax.rem(z + d, 16))).start()
        return 0

    lax.fori_loop(1, 16, top_to_z, 0)
    relay_third(0, (2,))

    got = cols.at[lax.rem(a + 3, 4), w]
    took(got, z_recv.at[0])
    remote(half(got, 0), half(got, 0), z_send, z_recv.at[2], ahead).start()
    send_own(3, got)
    got = cols.at[lax.rem(a + 1, 4), w]
    took(got, z_recv.at[1])
    remote(half(got, 1), half(got, 1), z_send, z_recv.at[2], back).start()
    send_own(1, got)
    finish(0)

    took(top_z.at[pl.ds(0, 15)], top_recv.at[0])
    top[1] = jnp.maximum(top[0], jnp.max(top_z[...], axis=0))

    def top_to_w(d, _):
        remote(top.at[1], top_w.at[d - 1], top_send.at[1], top_recv.at[1], (lax.rem(w + d, 32), z)).start()
        return 0

    lax.fori_loop(1, 32, top_to_w, 0)

    relay_first(3)
    relay_first(1)
    relay_second(3)
    relay_second(1)
    got = cols.at[lax.rem(a + 2, 4), w]
    took(got, z_recv.at[2])
    send_own(2, got)
    relay_rows(1)
    relay_third(3, (0, 1, 2))
    relay_third(1, (0, 1, 2))
    relay_first(2)
    relay_second(2)
    relay_rows(2)
    finish(3)
    finish(1)
    relay_third(2, (0, 1, 2))
    finish(2)
    relay_rows(3)

    took(top_w.at[pl.ds(0, 31)], top_recv.at[1])
    peak_out[...] = jnp.maximum(top[1], jnp.max(top_w[...], axis=0))
    small_out[...] = small_all[...]

    for one in keep:
        one.wait()
    took(cols.at[pl.ds(0, 2)], core_recv)
    took(cols.at[pl.ds(0, 2)], core_send)
    for k in range(4):
        took(cols.at[0, pl.ds(0, 15)], xy_send.at[k])
    took(cols.at[0, pl.ds(0, 3)], z_send)
    took(small_all.at[pl.ds(0, 3)], small_send)
    took(top_z.at[pl.ds(0, 15)], top_send.at[0])
    took(top_w.at[pl.ds(0, 31)], top_send.at[1])
    for d in range(3):

        @pl.when((b >= d) & (b < 3))
        def _():
            took(rows.at[0], row_send.at[0, d])

        @pl.when((b + d <= 3) & (b > 0))
        def _():
            took(rows.at[0], row_send.at[1, d])


def gather(wk, em, small):
    f32 = jnp.float32
    return pl.pallas_call(
        gather_kernel,
        out_shape=[
            jax.ShapeDtypeStruct((4, RW, E), jnp.bfloat16),
            jax.ShapeDtypeStruct((4, 32, 2, 16, 2048), jnp.bfloat16),
            jax.ShapeDtypeStruct((4, 24, 128), f32),
            jax.ShapeDtypeStruct((8, 128), f32),
        ],
        in_specs=[ANY, ANY, VMEM],
        out_specs=[ANY, ANY, VMEM, VMEM],
        scratch_shapes=[
            pltpu.VMEM((4, 24, 128), f32),
            pltpu.VMEM((2, 8, 128), f32),
            pltpu.VMEM((15, 8, 128), f32),
            pltpu.VMEM((31, 8, 128), f32),
            DMA((2,)), DMA, DMA((3,)), DMA((4,)), DMA((4, 19)), DMA, DMA,
            DMA((2, 3)), DMA((2, 3, CHUNKS)), DMA, DMA, DMA((2,)), DMA((2,)),
        ],
        compiler_params=pltpu.CompilerParams(collective_id=0, has_side_effects=True),
        name="gather",
    )(wk, em, small)


def build_kernel(row_s, plane_s, col_s, count_s, row_ref, col_ref, tile_ref):
    t = pl.program_id(0)

    @pl.when(t < count_s[0])
    def _():
        both = col_ref[...].reshape(32, 16, RE).astype(jnp.float32)
        upper = (col_s[t] // 16) == 1
        cols = jnp.where(upper, both[:, 8:, :], both[:, :8, :]).reshape(E, RE)
        inv_cols = lax.rsqrt(jnp.sum(cols * cols, axis=0, keepdims=True) * (1.0 / E) + EPSILON)
        cols = cols.astype(jnp.bfloat16)
        for j in range(4):
            part = row_ref[0, pl.ds(j * 256, 256), :]
            wide = part.astype(jnp.float32)
            inv_rows = lax.rsqrt(jnp.sum(wide * wide, axis=1, keepdims=True) * (1.0 / E) + EPSILON)
            cosine = jnp.dot(part, cols, preferred_element_type=jnp.float32)
            cosine = cosine * inv_rows * inv_cols * (1.0 / E)
            tile_ref[0, pl.ds(j * 256, 256), :] = jnp.exp((cosine - 1.0) * (1.0 / SOFTMAX_TEMP)).astype(jnp.bfloat16)

    @pl.when(t >= count_s[0])
    def _():
        tile_ref[...] = jnp.zeros_like(tile_ref)


def build(slots, row, plane, col, count, rows, cols):
    return pl.pallas_call(
        build_kernel,
        out_shape=jax.ShapeDtypeStruct((slots, RW, RE), jnp.bfloat16),
        grid_spec=pltpu.PrefetchScalarGridSpec(
            num_scalar_prefetch=4,
            grid=(slots,),
            in_specs=[
                pl.BlockSpec((1, RW, E), lambda t, r, p, k, n: (r[t], 0, 0)),
                pl.BlockSpec(
                    (1, 32, 1, 16, RE),
                    lambda t, r, p, k, n: (p[t], 0, lax.rem(k[t] // 8, 2), 0, lax.rem(k[t], 8)),
                ),
            ],
            out_specs=pl.BlockSpec((1, RW, RE), lambda t, r, p, k, n: (t, 0, 0)),
        ),
        compiler_params=pltpu.CompilerParams(dimension_semantics=("arbitrary",)),
        name="build_tiles",
    )(row, plane, col, count, rows, cols)


def pick(block, line):
    at = lax.broadcasted_iota(jnp.int32, block.shape, 0)
    first = jnp.sum(jnp.where(at == 2 * line, block, 0.0), axis=0, keepdims=True)
    second = jnp.sum(jnp.where(at == 2 * line + 1, block, 0.0), axis=0, keepdims=True)
    return jnp.concatenate([first, second], axis=1)


def in_two(vector):
    wide = jnp.broadcast_to(vector, (16, vector.shape[1]))
    high = wide.astype(jnp.bfloat16).astype(jnp.float32)
    at = lax.broadcasted_iota(jnp.int32, wide.shape, 0)
    return jnp.where(at == 0, high, jnp.where(at == 1, wide - high, 0.0)).astype(jnp.bfloat16)


def iterate_kernel(
    slots,
    row_s, plane_s, col_s, tiles, spots, worker_mass, employer_mass,
    worker_out, employer_out,
    row_buf, part, col_own, col_buf, plane_buf, scale_buf, out_buf,
    row_send, row_recv, col_send, col_recv, plane_send, plane_recv,
    scale_send, scale_recv, out_send, out_recv,
):
    x, y, c, a, b = place()
    w, z = lax.axis_index("wrk"), lax.axis_index("emp")
    barrier = pltpu.get_barrier_semaphore()

    def greet_w(d, _):
        pl.semaphore_signal(barrier, inc=1, device_id=(lax.rem(w + d, 32), z), device_id_type=MESH)
        return 0

    lax.fori_loop(1, 32, greet_w, 0)
    for d in (1, 2, 3):
        pl.semaphore_signal(barrier, inc=1, device_id=(w, lax.rem(z + 4 * d, 16)), device_id_type=MESH)
        pl.semaphore_signal(barrier, inc=1, device_id=(w, 4 * a + lax.rem(b + d, 4)), device_id_type=MESH)

    row_line = lax.broadcasted_iota(jnp.int32, (8, 512), 0)
    spot = lax.broadcasted_iota(jnp.int32, (256, slots), 0)

    for it in range(ITERS):

        def row_step(t, total):
            if it == 0:
                scale = jnp.ones((1, RE), jnp.float32)
            else:
                scale = pick(scale_buf[it - 1, col_s[t]], plane_s[t])
            sums = lax.dot_general(
                in_two(scale), tiles[t], (((1,), (1,)), ((), ())), preferred_element_type=jnp.float32
            )
            sums = sums[0:1] + sums[1:2]
            line = 2 * row_s[t]
            total = total + jnp.where(row_line == line, sums[:, :512], 0.0)
            return total + jnp.where(row_line == line + 1, sums[:, 512:], 0.0)

        row_buf[it, b] = lax.fori_loop(0, slots, row_step, jnp.zeros((8, 512), jnp.float32))
        if it == 0:
            pl.semaphore_wait(barrier, 37)
        for d in (1, 2, 3):
            mine = row_buf.at[it, b]
            remote(mine, mine, row_send.at[it], row_recv.at[it], (w, 4 * a + lax.rem(b + d, 4))).start()
        took(row_buf.at[it, pl.ds(0, 3)], row_recv.at[it])
        row_total = (row_buf[it, 0] + row_buf[it, 1]) + (row_buf[it, 2] + row_buf[it, 3])
        worker_scale = worker_mass[a] / row_total
        if it == ITERS - 1:
            out_buf[a] = SOFTMAX_TEMP * jnp.log(worker_scale)
            for d in (1, 2, 3):
                remote(out_buf.at[a], out_buf.at[a], out_send, out_recv, (w, lax.rem(z + 4 * d, 16))).start()

        def col_step(t, _):
            scale = pick(worker_scale, row_s[t])
            sums = jnp.dot(in_two(scale), tiles[t], preferred_element_type=jnp.float32)
            part[t] = sums[0:1] + sums[1:2]
            return 0

        lax.fori_loop(0, slots, col_step, 0)
        sums = part[...].reshape(slots, RE)
        totals = jnp.dot(
            jnp.where(spot == spots[0:1, :slots], 1.0, 0.0), sums[:, :128],
            precision=lax.Precision.HIGHEST, preferred_element_type=jnp.float32,
        ) + jnp.dot(
            jnp.where(spot == spots[0:1, :slots] + 1, 1.0, 0.0), sums[:, 128:],
            precision=lax.Precision.HIGHEST, preferred_element_type=jnp.float32,
        )
        col_own[it] = totals.reshape(32, 8, 128)

        def scatter(d, _):
            to = lax.rem(w + d, 32)
            remote(col_own.at[it, to], col_buf.at[it, d - 1], col_send.at[it], col_recv.at[it], (to, z)).start()
            return 0

        lax.fori_loop(1, 32, scatter, 0)
        took(col_buf.at[it], col_recv.at[it])
        plane_buf[it, a] = col_own[it, w] + jnp.sum(col_buf[it], axis=0)
        for d in (1, 2, 3):
            mine = plane_buf.at[it, a]
            remote(mine, mine, plane_send.at[it], plane_recv.at[it], (w, lax.rem(z + 4 * d, 16))).start()
        took(plane_buf.at[it, pl.ds(0, 3)], plane_recv.at[it])
        column_total = (plane_buf[it, 0] + plane_buf[it, 1]) + (plane_buf[it, 2] + plane_buf[it, 3])
        scale_buf[it, w] = employer_mass[...] / column_total

        def share(d, _):
            mine = scale_buf.at[it, w]
            remote(mine, mine, scale_send.at[it], scale_recv.at[it], (lax.rem(w + d, 32), z)).start()
            return 0

        lax.fori_loop(1, 32, share, 0)
        took(scale_buf.at[it, pl.ds(0, 31)], scale_recv.at[it])

    employer_out[...] = SOFTMAX_TEMP * jnp.log(scale_buf[ITERS - 1])
    took(out_buf.at[pl.ds(0, 3)], out_recv)
    worker_out[...] = out_buf[...]

    took(out_buf.at[pl.ds(0, 3)], out_send)
    for it in range(ITERS):
        took(row_buf.at[it, pl.ds(0, 3)], row_send.at[it])
        took(col_buf.at[it], col_send.at[it])
        took(plane_buf.at[it, pl.ds(0, 3)], plane_send.at[it])
        took(scale_buf.at[it, pl.ds(0, 31)], scale_send.at[it])


def iterate(slots, cid, row, plane, col, tiles, spots, worker_mass, employer_mass):
    f32 = jnp.float32
    return pl.pallas_call(
        functools.partial(iterate_kernel, slots),
        out_shape=[jax.ShapeDtypeStruct((4, 8, 512), f32), jax.ShapeDtypeStruct((32, 8, 128), f32)],
        in_specs=[SMEM, SMEM, SMEM, VMEM, VMEM, VMEM, VMEM],
        out_specs=[VMEM, VMEM],
        scratch_shapes=[
            pltpu.VMEM((ITERS, 4, 8, 512), f32),
            pltpu.VMEM((slots, 1, RE), f32),
            pltpu.VMEM((ITERS, 32, 8, 128), f32),
            pltpu.VMEM((ITERS, 31, 8, 128), f32),
            pltpu.VMEM((ITERS, 4, 8, 128), f32),
            pltpu.VMEM((ITERS, 32, 8, 128), f32),
            pltpu.VMEM((4, 8, 512), f32),
        ]
        + [DMA((ITERS,))] * 8
        + [DMA, DMA],
        compiler_params=pltpu.CompilerParams(
            collective_id=cid, has_side_effects=True, vmem_limit_bytes=44 << 20
        ),
        name=f"iterate_{slots}",
    )(row, plane, col, tiles, spots, worker_mass, employer_mass)


def shards(worker_emb, employer_emb, eligible, worker_mass, employer_mass):
    a = lax.axis_index("emp") // 4
    w = lax.axis_index("wrk")
    em = employer_emb.reshape(8, 2, 2, 2048).transpose(2, 1, 0, 3).reshape(2, 16, 2048)
    mass = lax.dynamic_slice_in_dim(employer_mass, w * RE, RE, 0).reshape(2, 128)
    small = jnp.concatenate(
        [
            jnp.pad(mass, ((0, 6), (0, 0))),
            jnp.pad(eligible.astype(jnp.float32), ((0, 0), (0, 96))),
        ],
        axis=0,
    )
    rows, cols, small_all, peak = gather(worker_emb, em, small)

    flags = lax.dynamic_slice_in_dim(small_all[:, 8:, :32], 4 * a, 4, 1).reshape(512)
    order = jnp.cumsum(flags.astype(jnp.int32))
    count = order[511:]
    most = SLOTS[-1]
    slot = jnp.minimum(jnp.arange(most, dtype=jnp.int32), jnp.maximum(count[0] - 1, 0))
    index = jnp.minimum(jnp.sum((order[None, :] <= slot[:, None]).astype(jnp.int32), axis=1), 511)
    plane, row, col = index // 128, index // 32 % 4, index % 32
    spots = jnp.broadcast_to((col * 8 + plane * 2)[None, :], (8, most))
    masses = small_all[:, :2, :].reshape(8, 128)

    def run(slots, cid):
        def branch():
            tiles = build(slots, row, plane, col, count, rows, cols)
            return iterate(
                slots, cid, row, plane, col, tiles, spots, worker_mass.reshape(4, 8, 512), masses
            )

        return branch

    worker_pot, employer_pot = lax.cond(peak[0, 0] <= SLOTS[0], run(SLOTS[0], 1), run(SLOTS[1], 2))
    employer_pot = lax.dynamic_slice_in_dim(employer_pot, 2 * a, 2, 1)
    return worker_pot.reshape(-1), employer_pot.reshape(-1)


def solution(mesh):
    return jax.shard_map(
        shards,
        mesh=mesh,
        in_specs=(P(("wrk", "emp"), None), P("wrk", "emp"), P("wrk", "emp"), P("wrk"), P("emp")),
        out_specs=(P("wrk"), P("emp")),
        check_vma=False,
    )
```

time: 1140 us -> 208 us (0.18)
  waiting for transfers between devices: 527 us -> 0 us
  blocking collectives: 389 us -> 0 us
  Pallas kernels: 0 us -> 194 us
  matrix products: 144 us -> 0 us
  local copies, waits for them, and re-layouts: 29.9 us -> 8.52 us
  loops' own time: 17.5 us -> 0.1 us
  other arithmetic: 16 us -> 2.56 us
  between operations: 14.1 us -> 2.1 us
    psum x3 -> x0, blocking collectives: 389 us -> none  [shards(): column_total = lax.psum(col_local, 'wrk')]
    psum x3 -> x0, waiting for transfers between devices: 357 us -> none  [shards(): row_total = lax.psum(row_local, 'emp')]
    pallas_call x0 -> x3, Pallas kernels: none -> 194 us  [the longest x1 92.3 us: gather(): pl.pallas_call(gather_kernel, out_shape=[jax.ShapeDtypeStruct((4, RW, E),...]
    all_gather x2 -> x0, waiting for transfers between devices: 168 us -> none  [the longest x1 104 us: shards(): worker_rows = lax.all_gather(worker_emb, 'emp', axis=0, tiled=True)]
    dot_general x96 -> x0, matrix products: 144 us -> none  [the longest x36 55.8 us: row_product(): jnp.dot(fetch(packed).astype(jnp.float32), packed[-1], precision=highest)]
    dynamic_slice x60 -> x1, local copies, waits for them, and re-layouts: 22.1 us -> 0.64 us  [shards(): employer_pot = lax.dynamic_slice_in_dim(employer_pot, 2 * a, 2, 1)]
    another operation x7 -> x1, loops' own time: 17.5 us -> 0.1 us  [shards(): lax.cond(peak[0, 0] <= SLOTS[0], run(SLOTS[0], 1), run(SLOTS[1], 2))]
  transfers between devices with their start and end apart: 5 -> 0, of which waited for: 5 -> 0; matrix products, arithmetic and copies ran while one was open for 1% -> 0% of each run, Pallas kernels for 0% -> 0%
where the time goes in v1:
time: 208 us; the launch traced here: 207 us
  Pallas kernels  194 us (93%)
  local copies, waits for them, and re-layouts  8.52 us (4%)
  other arithmetic  2.56 us (1%)
  between operations  2.1 us (1%)
    pallas_call x1, Pallas kernels, gather(): pl.pallas_call(gather_kernel, out_shape=[jax.ShapeDtypeStruct((4, RW, E),...  92.3 us
    pallas_call x1, Pallas kernels, iterate(): pl.pallas_call(functools.partial(iterate_kernel, slots), out_shape=[jax.S...  89.6 us
    pallas_call x1, Pallas kernels, build(): pl.pallas_call(build_kernel, out_shape=jax.ShapeDtypeStruct((slots, RW, R...  11.8 us

profile of v1, /device:TPU:1, one launch (start us, length us, event | category | flops | bytes accessed | tf_op | source)
XLA Modules:
  0.0 207.0 jit_solution(13878623220046131899)
XLA Ops:
  0.6 0.0 copy-start
  0.7 0.7 copy-done
  1.4 0.1 dynamic-slice_bitcast_fusion
  1.5 0.7 convert_element_type.23
  2.2 0.6 select_maximum_fusion.small
  2.8 1.6 copy.13
  4.3 92.3 %gather.1 = (bf16[4,1024,256]{2,1,0:T(8,128)(2,1)S(1)}, bf16[4,32,2,16,2048]{4,3,2,1,0:T(8,128)(2,1)}, f32[4,24,128]{2,1,0:T(8,128)S(1)}, f32[8,128]{1,0:T(8,128)}) custom-call(bf16[1024,256]{1,0:T(8,128)(2,1)} %wk.1, bf16[2,16,2048]{2,1,0:T(8,128)(2,1)} %bitcast.43, f32[24,128]{1,0:T(8,128)} %select_maximum_fusion.small), custom_call_target="tpu_custom_call" | custom-call | tf_op jit(solution)/shard_map/gather/pallas_call | solution.py:273
  96.7 1.2 slice.25
  98.6 0.1 convert_element_type.27
  98.7 0.3 reduce-window.9
  99.0 0.1 slice.27
  99.1 0.1 slice_reduce_fusion
  99.2 0.1 add_bitcast_fusion.2
  99.3 0.6 slice.29
  100.5 0.2 convert_reduce_fusion
  100.8 105.5 %conditional.1 = (f32[32,8,128]{2,1,0:T(8,128)S(1)}, f32[16384]{0:T(1024)S(1)}) conditional(s32[]{:T(128)} %bitcast.8, (s32[48]{0:T(128)S(1)}, s32[48]{0:T(128)S(1)}, s32[48]{0:T(128)S(1)}, s32[48]{0:T(128)S(1)}, pred[48]{0:T(512)(128)(4,1)S(1)}, /*index=5*/pred[48]{0:T(512)(128)(4,1)S(1)}, s32[48]{0:T(128)S(1)}, s32[48]{0:T(128)S(1)}, ...), branch_computations={%region_3.4_spmd, %region_4.5_spmd} | conditional | flops 1536 | bytes 34094700 | solution.py:517
  100.8 0.0 copy-start.8
  100.9 0.6 and_select_fusion.7
  101.5 0.0 copy-start.2
  101.5 0.0 copy-start.3
  101.5 0.0 copy-start.4
  101.5 11.8 %build_tiles.3.tiles = bf16[16,1024,256]{2,1,0:T(8,128)(2,1)} custom-call(s32[48]{0:T(128)} %get-tuple-element.452.row_s, s32[48]{0:T(128)} %get-tuple-element.451.plane_s, s32[48]{0:T(128)} %get-tuple-element.450.col_s, s32[1]{0:T(128)} %get-tuple-element.419.count_s, bf16[4,1024,256]{2,1,0:T(8,128)(2,1)S(1)} %get-tuple-element.420.row_ref, ...), custom_call_target="tpu_custom_call" | custom-call | tf_op jit(solution)/shard_map/cond/branch_1_fun/build_tiles/pallas_call | solution.py:320
  113.3 0.0 copy-done.8
  113.4 0.0 copy-done.2
  113.4 0.0 copy-done.3
  113.4 0.0 copy-done.4
  113.4 0.0 copy-start.1
  113.4 3.4 %copy-done.1 = bf16[16,1024,256]{2,1,0:T(8,128)(2,1)S(1)} copy-done((bf16[16,1024,256]{2,1,0:T(8,128)(2,1)S(1)}, bf16[16,1024,256]{2,1,0:T(8,128)(2,1)}, u32[]{:S(2)}) %copy-start.1) | copy-done | bytes 8388632 | tf_op jit(solution)/shard_map/cond
  116.8 89.6 %iterate_16.2 = (f32[4,8,512]{2,1,0:T(8,128)S(1)}, f32[32,8,128]{2,1,0:T(8,128)S(1)}) custom-call(s32[48]{0:T(128)S(1)} %copy-done.4, s32[48]{0:T(128)S(1)} %copy-done.3, s32[48]{0:T(128)S(1)} %copy-done.2, bf16[16,1024,256]{2,1,0:T(8,128)(2,1)S(1)} %copy-done.1, s32[8,48]{1,0:T(8,128)S(1)} %broadcast_in_dim.21.spots, ...), custom_call_target="tpu_custom_call" | custom-call | tf_op jit(solution)/shard_map/cond/branch_1_fun/iterate_16/pallas_call | solution.py:461
  206.4 0.0 copy-start.9
  206.4 0.6 constant_dynamic-slice_fusion
  207.0 0.0 copy-done.9
  (19 shorter events, 0.2 us)
Async XLA Ops:
  0.6 0.8 copy-start
  100.8 12.5 %copy-start.8 = (f32[16384]{0:T(1024)S(1)}, f32[16384]{0:T(1024)}, u32[]{:S(2)}) copy-start(f32[16384]{0:T(1024)} %get-tuple-element.429) | copy-start | bytes 196612 | tf_op jit(solution)/shard_map/cond
  101.5 11.9 %copy-start.2 = (s32[48]{0:T(128)S(1)}, s32[48]{0:T(128)}, u32[]{:S(2)}) copy-start(s32[48]{0:T(128)} %get-tuple-element.450.col_s) | copy-start | bytes 580 | tf_op jit(solution)/shard_map/cond
  101.5 11.9 %copy-start.3 = (s32[48]{0:T(128)S(1)}, s32[48]{0:T(128)}, u32[]{:S(2)}) copy-start(s32[48]{0:T(128)} %get-tuple-element.451.plane_s) | copy-start | bytes 580 | tf_op jit(solution)/shard_map/cond
  101.5 11.9 %copy-start.4 = (s32[48]{0:T(128)S(1)}, s32[48]{0:T(128)}, u32[]{:S(2)}) copy-start(s32[48]{0:T(128)} %get-tuple-element.452.row_s) | copy-start | bytes 580 | tf_op jit(solution)/shard_map/cond
  113.4 3.4 %copy-start.1 = (bf16[16,1024,256]{2,1,0:T(8,128)(2,1)S(1)}, bf16[16,1024,256]{2,1,0:T(8,128)(2,1)}, u32[]{:S(2)}) copy-start(bf16[16,1024,256]{2,1,0:T(8,128)(2,1)} %build_tiles.3.tiles) | copy-start | bytes 25165828 | tf_op jit(solution)/shard_map/cond
  206.4 0.7 copy-start.9

commit v2 on v0

v2 whole, which is shorter than its diff:
```python
import functools

import jax
import jax.numpy as jnp
from jax import lax
from jax.experimental import pallas as pl
from jax.experimental.pallas import tpu as pltpu
from jax.sharding import PartitionSpec as P

E = 256
ITERS = 3
SOFTMAX_TEMP = 0.25
EPSILON = 1e-06
RW = 1024
RE = 256
SLOTS = (13, 17, 48)
CHUNKS = 4
ORDER = (
    "Z", "o0", "o1", "f00", "f01", "f02", "f03", "f10", "f11", "f12", "f13", "s00", "s01", "R", "s10", "s11",
    "o2", "o3", "t00", "t01", "t02", "t03", "t10", "t11", "t12", "t13", "f20", "f21", "f22", "f23", "f30", "o4",
    "o5", "f31", "f32", "f33", "r10", "e0", "s21", "s20", "e1", "r11", "f40", "f41", "f42", "f43", "f51", "s30",
    "s31", "f50", "f52", "f53", "r12", "t20", "t21", "t22", "t23", "s40", "s41", "r13", "t30", "t31", "t32",
    "t33", "s50", "s51", "e2", "t40", "t41", "t42", "t43", "o6", "o7", "m0", "r20", "e3", "t50", "t51", "t52",
    "t53", "r21", "m1", "e4", "f60", "f61", "f62", "f63", "f70", "f71", "f72", "f73", "r22", "e5", "s60", "s61",
    "m2", "s70", "s71", "r23", "m3", "r30", "t60", "t61", "t62", "t63", "r31", "m4", "t70", "t71", "t72", "t73",
    "e6", "r32", "m5", "e7", "r33", "m6", "m7",
)
MESH = pl.DeviceIdType.MESH
VMEM = pl.BlockSpec(memory_space=pltpu.VMEM)
SMEM = pl.BlockSpec(memory_space=pltpu.SMEM)
HBM = pl.BlockSpec(memory_space=pltpu.HBM)
DMA = pltpu.SemaphoreType.DMA


def place():
    w, z = lax.axis_index("wrk"), lax.axis_index("emp")
    return w // 8, lax.rem(w // 2, 4), lax.rem(w, 2), z // 4, lax.rem(z, 4)


def device(x, y, c, z):
    return ((lax.rem(x, 4) * 4 + lax.rem(y, 4)) * 2 + c, lax.rem(z, 16))


def remote(src, dst, send, recv, to):
    return pltpu.make_async_remote_copy(
        src_ref=src, dst_ref=dst, send_sem=send, recv_sem=recv, device_id=to, device_id_type=MESH
    )


def took(ref, sem):
    pltpu.make_async_copy(ref, ref, sem).wait()


def gather_kernel(
    wk, em_all, eligible_all, mass_all,
    rows, cols, lists, spots, masses, peak,
    em, eligible, mass, shard, small_all, top, top_all,
    load_sem, keep_sem, z_send, z_recv, xy_send, xy_recv, core_send, core_recv,
    row_send, row_recv, small_send, small_recv, top_send, top_recv,
):
    x, y, c, a, b = place()
    w, z = lax.axis_index("wrk"), lax.axis_index("emp")
    left, right = device(x + 3, y, c, z), device(x + 1, y, c, z)
    down, up = device(x, y + 3, c, z), device(x, y + 1, c, z)
    back, ahead = (w, lax.rem(z + 12, 16)), (w, lax.rem(z + 4, 16))
    twin = (w + 1 - 2 * c, z)

    loads = [
        pltpu.make_async_copy(src, dst, load_sem.at[k])
        for k, (src, dst) in enumerate(((em_all, em), (eligible_all, eligible), (mass_all, mass)))
    ]
    for one in loads:
        one.start()
    top_all[...] = jnp.zeros_like(top_all)
    barrier = pltpu.get_barrier_semaphore()
    beside = [(w, 4 * a + lax.rem(b + d, 4)) for d in (1, 3)]
    for to in (left, right, down, up, back, ahead, twin, *beside):
        pl.semaphore_signal(barrier, inc=1, device_id=to, device_id_type=MESH)

    for one in loads:
        one.wait()
    for k in range(2):
        for g in range(2):
            at = 2048 * g + 1024 * k
            for q in range(4):
                here = at + RE * q
                shard[k, g, q] = jnp.concatenate(
                    [em[:, here : here + RE], em[:, 4096 + here : 4096 + here + RE]], axis=0
                )
    small_all[a] = jnp.zeros((24, 128), jnp.float32)
    small_all[a, 0:2, :] = mass[pl.ds(2 * w, 2), :]
    small_all[a, 8:24, 0:32] = eligible[...].astype(jnp.float32)
    keep = [
        pltpu.make_async_copy(shard, cols.at[a, :, x, y, c], keep_sem.at[0]),
        pltpu.make_async_copy(wk, rows.at[b], keep_sem.at[1]),
    ]
    for one in keep:
        one.start()
    pl.semaphore_wait(barrier, 9)

    xs = [lax.rem(x + i, 4) for i in range(4)]
    ys = [lax.rem(y + i, 4) for i in range(4)]
    ps = [lax.rem(a + i, 4) for i in range(4)]
    near = (right, left, up, down)

    def part(s):
        return cols.at[ps[(0, 0, 3, 1, 3, 1, 2, 2)[s]], (0, 1, 0, 0, 1, 1, 0, 1)[s]]

    def push(src, k, kind, sem):
        remote(src, src, xy_send.at[kind, k], sem, near[k]).start()

    def lanes(ref, k):
        return ref.at[pl.ds(2 * k, 2)] if len(ref.shape) == 3 else ref.at[:, pl.ds(2 * k, 2)]

    def z_own():
        for k in range(2):
            for g, to in enumerate((ahead, back)):
                remote(shard.at[k], cols.at[a, k, x, y, c], z_send, z_recv.at[g, k], to).start()
            if k == 0:
                for g, to in enumerate((ahead, back)):
                    remote(small_all.at[a], small_all.at[a], small_send, small_recv.at[g], to).start()

    def own(s):
        got = part(s).at[x, y, c]
        if 2 <= s < 6:
            g, k = s % 2, s // 4
            took(got, z_recv.at[g, k])
            if g == k:
                remote(got, got, z_send, z_recv.at[2, k], (ahead, back)[g]).start()
            if s == 2:
                few = small_all.at[ps[3]]
                took(few, small_recv.at[0])
                remote(few, few, small_send, small_recv.at[2], ahead).start()
        if s >= 6:
            took(got, z_recv.at[2, s - 6])
        for k in range(4):
            src = shard.at[s, k // 2] if s < 2 else got.at[k // 2]
            remote(src, got.at[k // 2], xy_send.at[0, k], xy_recv.at[s, k], near[k]).start()
        if s == 1:
            keep[0].wait()

    def first(s, k):
        i, j = ((3, 0), (1, 0), (0, 3), (0, 1))[k]
        got = part(s).at[xs[i], ys[j], c, k // 2]
        took(got, xy_recv.at[s, k])
        push(lanes(got, k % 2), k, 1, xy_recv.at[s, 4 + k // 2])

    def second(s, axis):
        took(part(s).at[x, y, c, axis], xy_recv.at[s, 4 + axis])
        line = part(s).at[:, y, c, 0] if axis == 0 else part(s).at[x, :, c, 1]
        for k in range(2):
            push(line, 2 - 2 * axis + k, 2, xy_recv.at[s, 6 + 2 * axis + k])

    def third(s, k):
        line = part(s).at[:, ys[3 - 2 * k], c, 0] if k < 2 else part(s).at[xs[7 - 2 * k], :, c, 1]
        took(line, xy_recv.at[s, 6 + k])
        push(lanes(line, k % 2), (2, 3, 0, 1)[k], 3, xy_recv.at[s, 10 + k // 2])

    def finish(s):
        took(part(s).at[:, y, c, 0], xy_recv.at[s, 10])
        took(part(s).at[:, y, c, 0], xy_recv.at[s, 11])
        got = part(s).at[:, :, c]
        remote(got, got, core_send, core_recv, twin).start()

    def row_chunk(block, j):
        return block.at[pl.ds(j * (RW // CHUNKS), RW // CHUNKS)]

    def send_rows():
        for j in range(CHUNKS):
            src = row_chunk(wk, j)

            @pl.when(b < 3)
            def _():
                remote(src, row_chunk(rows.at[b], j), row_send.at[0, 0], row_recv.at[0, 0, j], (w, z + 1)).start()

            @pl.when(b > 0)
            def _():
                remote(src, row_chunk(rows.at[b], j), row_send.at[1, 0], row_recv.at[1, 0, j], (w, z - 1)).start()

    def relay(d, j):
        @pl.when(b >= d)
        def _():
            took(row_chunk(rows.at[b - d], j), row_recv.at[0, d - 1, j])

        if d < 3:

            @pl.when((b >= d) & (b < 3))
            def _():
                got = row_chunk(rows.at[b - d], j)
                remote(got, got, row_send.at[0, d], row_recv.at[0, d, j], (w, z + 1)).start()

        @pl.when(b + d <= 3)
        def _():
            took(row_chunk(rows.at[b + d], j), row_recv.at[1, d - 1, j])

        if d < 3:

            @pl.when((b + d <= 3) & (b > 0))
            def _():
                got = row_chunk(rows.at[b + d], j)
                remote(got, got, row_send.at[1, d], row_recv.at[1, d, j], (w, z - 1)).start()

    def list_tiles():
        took(small_all.at[0], small_recv.at[1])
        took(small_all.at[0], small_recv.at[2])
        masses[...] = small_all[:, 0:2, :].reshape(8, 128)
        flags = small_all[:, 8:24, :].reshape(64, 128)
        line = lax.broadcasted_iota(jnp.int32, (64, 128), 0)
        lane = lax.broadcasted_iota(jnp.int32, (64, 128), 1)
        group = lax.rem(line, 16) // 4
        most = jnp.zeros((1, 1), jnp.float32)
        for g in range(4):
            most = jnp.maximum(most, jnp.sum(jnp.where(group == g, flags, 0.0), keepdims=True))
        top[0] = jnp.broadcast_to(most, (8, 128))
        mine = jnp.where(group == a, flags, 0.0)
        upto = (
            lax.broadcasted_iota(jnp.int32, (128, 128), 0) <= lax.broadcasted_iota(jnp.int32, (128, 128), 1)
        ).astype(jnp.float32)
        above = (
            lax.broadcasted_iota(jnp.int32, (64, 64), 1) < lax.broadcasted_iota(jnp.int32, (64, 64), 0)
        ).astype(jnp.float32)
        before = jnp.sum(jnp.dot(above, mine, preferred_element_type=jnp.float32), axis=1, keepdims=True)
        order = jnp.dot(mine, upto, preferred_element_type=jnp.float32) + before
        slot = lane.astype(jnp.float32)
        ends = before + jnp.sum(mine, axis=1, keepdims=True)
        slot_line = jnp.sum(jnp.where(ends <= slot, 1.0, 0.0), axis=0, keepdims=True)
        hit = jnp.where(line.astype(jnp.float32) == slot_line, 1.0, 0.0)
        there = lax.dot_general(order, hit, (((0,), (0,)), ((), ())), preferred_element_type=jnp.float32)
        slot_lane = jnp.sum(jnp.where(there <= slot[0:1], 1.0, 0.0), axis=0, keepdims=True)
        count = jnp.sum(mine, keepdims=True)
        codes = jnp.where(slot[0:1] < count, slot_line * 32.0 + slot_lane, 0.0).astype(jnp.int32)
        count = jnp.broadcast_to(count, (1, 128)).astype(jnp.int32)
        plane, row, col = codes // 512, lax.rem(codes // 32, 4), lax.rem(codes, 32)
        at = lax.broadcasted_iota(jnp.int32, (8, 128), 0)
        fields = (
            row, plane, col, count, lax.rem(col // 4, 2), lax.rem(col // 8, 2), lax.rem(col, 4), col // 16,
        )
        table = jnp.zeros((8, 128), jnp.int32)
        for k, field in enumerate(fields):
            table = jnp.where(at == k, field, table)
        lists[...] = table
        spots[...] = jnp.broadcast_to(col * 8 + plane * 2, (8, 128))

    def top_send_to(k, g, to):
        remote(top.at[k], top_all.at[k, g], top_send.at[k, g], top_recv.at[k, g], to).start()

    def maximum(k):
        if k == 0:
            list_tiles()
        else:
            if k <= 4:
                for g in range(2):
                    took(top_all.at[k - 1, g], top_recv.at[k - 1, g])
            else:

                @pl.when(b > 0)
                def _():
                    took(top_all.at[k - 1, 0], top_recv.at[k - 1, 0])

                @pl.when(b < 3)
                def _():
                    took(top_all.at[k - 1, 1], top_recv.at[k - 1, 1])

            top[k] = jnp.maximum(top[k - 1], jnp.maximum(top_all[k - 1, 0], top_all[k - 1, 1]))
        if k < 4:
            for g in range(2):
                top_send_to(k, g, near[2 * (k // 2) + g])
        elif k < 7:

            @pl.when(b < 3)
            def _():
                top_send_to(k, 0, (w, z + 1))

            @pl.when(b > 0)
            def _():
                top_send_to(k, 1, (w, z - 1))

        else:
            top_send_to(k, 0, twin)

    steps = dict(
        m=maximum,
        Z=z_own, o=own, f=first, s=second, t=third, e=finish, R=send_rows, r=relay,
    )
    for step in ORDER:
        steps[step[0]](*map(int, step[1:]))

    took(top_all.at[7, 0], top_recv.at[7, 0])
    peak[...] = jnp.maximum(top[7], top_all[7, 0])

    keep[1].wait()
    took(cols.at[pl.ds(0, 2)], core_recv)
    took(cols.at[pl.ds(0, 2)], core_send)
    for k in range(4):
        took(cols.at[0, 0, 0, pl.ds(0, 2)], xy_send.at[0, k])
        took(cols.at[0, 0, 0, 0], xy_send.at[1, k])
        took(cols.at[0, 0, pl.ds(0, 2)], xy_send.at[2, k])
        took(cols.at[0, 0, 0], xy_send.at[3, k])
    took(cols.at[0, 0, 0, pl.ds(0, 3)], z_send)
    took(small_all.at[pl.ds(0, 3)], small_send)
    for k in range(4):
        for g in range(2):
            took(top.at[k], top_send.at[k, g])
    took(top.at[7], top_send.at[7, 0])
    for k in range(4, 7):

        @pl.when(b < 3)
        def _():
            took(top.at[k], top_send.at[k, 0])

        @pl.when(b > 0)
        def _():
            took(top.at[k], top_send.at[k, 1])

    for d in range(3):

        @pl.when((b >= d) & (b < 3))
        def _():
            took(rows.at[0], row_send.at[0, d])

        @pl.when((b + d <= 3) & (b > 0))
        def _():
            took(rows.at[0], row_send.at[1, d])


def gather(wk, em, eligible, mass):
    f32 = jnp.float32
    return pl.pallas_call(
        gather_kernel,
        out_shape=[
            jax.ShapeDtypeStruct((4, RW, E), jnp.bfloat16),
            jax.ShapeDtypeStruct((4, 2, 4, 4, 2, 2, 4, 16, RE), jnp.bfloat16),
            jax.ShapeDtypeStruct((8, 128), jnp.int32),
            jax.ShapeDtypeStruct((8, 128), jnp.int32),
            jax.ShapeDtypeStruct((8, 128), f32),
            jax.ShapeDtypeStruct((8, 128), f32),
        ],
        in_specs=[HBM] * 4,
        out_specs=[VMEM] * 6,
        scratch_shapes=[
            pltpu.VMEM((8, 8192), jnp.bfloat16),
            pltpu.VMEM((16, 32), jnp.int32),
            pltpu.VMEM((64, 128), f32),
            pltpu.VMEM((2, 2, 4, 16, RE), jnp.bfloat16),
            pltpu.VMEM((4, 24, 128), f32),
            pltpu.VMEM((8, 8, 128), f32),
            pltpu.VMEM((8, 2, 8, 128), f32),
            DMA((3,)), DMA((2,)), DMA, DMA((3, 2)), DMA((4, 4)), DMA((8, 12)), DMA, DMA,
            DMA((2, 3)), DMA((2, 3, CHUNKS)), DMA, DMA((3,)), DMA((8, 2)), DMA((8, 2)),
        ],
        compiler_params=pltpu.CompilerParams(collective_id=0, has_side_effects=True, vmem_limit_bytes=24 << 20),
        name="gather",
    )(wk, em, eligible, mass)


def build_tile(t, lists, rows, cols, tiles):
    row = lists[0, t]
    keep = jnp.where(jnp.full((1, RE), lists[3, t], jnp.int32) > t, 1.0, 0.0)
    both = cols[lists[1, t], lists[4, t], :, :, :, lists[5, t], lists[6, t], :, :]
    both = both.reshape(32, 16, RE).astype(jnp.float32)
    upper = jnp.full((32, 8, RE), lists[7, t], jnp.int32) == 1
    side = jnp.where(upper, both[:, 8:, :], both[:, :8, :]).reshape(E, RE)
    inv_cols = lax.rsqrt(jnp.sum(side * side, axis=0, keepdims=True) * (1.0 / E) + EPSILON)
    inv_cols = inv_cols * (1.0 / E)
    side = side.astype(jnp.bfloat16)
    for j in range(RW // 256):
        part = rows[row, pl.ds(j * 256, 256), :]
        wide = part.astype(jnp.float32)
        inv_rows = lax.rsqrt(jnp.sum(wide * wide, axis=1, keepdims=True) * (1.0 / E) + EPSILON)
        cosine = jnp.dot(part, side, preferred_element_type=jnp.float32) * inv_rows * inv_cols
        value = jnp.exp((cosine - 1.0) * (1.0 / SOFTMAX_TEMP)) * keep
        tiles[t, pl.ds(j * 256, 256), :] = value.astype(jnp.bfloat16)


def in_line(block, lines):
    return jnp.concatenate([jnp.broadcast_to(block[k : k + 1], (16, 128)) for k in lines], axis=1)


def stacked(vector):
    at = lax.broadcasted_iota(jnp.int32, (8, 128), 0)
    out = jnp.zeros((8, 128), jnp.float32)
    for k in range(8):
        out = jnp.where(at == k, vector[:, 128 * k : 128 * k + 128], out)
    return out


def in_two(wide):
    high = wide.astype(jnp.bfloat16).astype(jnp.float32)
    at = lax.broadcasted_iota(jnp.int32, wide.shape, 0)
    return jnp.where(at == 0, high, jnp.where(at == 1, wide - high, 0.0)).astype(jnp.bfloat16)


def iterate_kernel(
    slots,
    lists, rows, cols, spots, worker_mass, employer_mass,
    worker_out, employer_out,
    tiles, row_buf, worker_scale, part, col_own, col_buf, plane_buf, scale_buf, out_buf,
    row_send, row_recv, col_send, col_recv, plane_send, plane_recv,
    scale_send, scale_recv, out_send, out_recv,
):
    x, y, c, a, b = place()
    w, z = lax.axis_index("wrk"), lax.axis_index("emp")
    barrier = pltpu.get_barrier_semaphore()

    def greet_w(d, _):
        pl.semaphore_signal(barrier, inc=1, device_id=(lax.rem(w + d, 32), z), device_id_type=MESH)
        return 0

    lax.fori_loop(1, 32, greet_w, 0)
    for d in (1, 2, 3):
        pl.semaphore_signal(barrier, inc=1, device_id=(w, lax.rem(z + 4 * d, 16)), device_id_type=MESH)
        pl.semaphore_signal(barrier, inc=1, device_id=(w, 4 * a + lax.rem(b + d, 4)), device_id_type=MESH)

    def build_step(t, _):
        build_tile(t, lists, rows, cols, tiles)
        return 0

    lax.fori_loop(0, slots, build_step, 0)
    unroll = slots if slots <= 20 else 4
    spot = lax.broadcasted_iota(jnp.int32, (256, slots), 0)
    block_line = lax.broadcasted_iota(jnp.int32, (8, 128), 0)

    for it in range(ITERS):

        def row_step(t, totals):
            if it == 0:
                scale = jnp.ones((16, RE), jnp.float32)
            else:
                block = scale_buf[it - 1, lists[2, t]]
                line = 2 * lists[1, t]
                first = jnp.sum(jnp.where(block_line == line, block, 0.0), axis=0, keepdims=True)
                second = jnp.sum(jnp.where(block_line == line + 1, block, 0.0), axis=0, keepdims=True)
                scale = jnp.broadcast_to(jnp.concatenate([first, second], axis=1), (16, RE))
            sums = lax.dot_general(
                in_two(scale), tiles[t], (((1,), (1,)), ((), ())), preferred_element_type=jnp.float32
            )
            sums = stacked(sums[0:1] + sums[1:2])
            row = jnp.full((8, 128), lists[0, t], jnp.int32)
            return tuple(total + jnp.where(row == r, sums, 0.0) for r, total in enumerate(totals))

        totals = lax.fori_loop(0, slots, row_step, (jnp.zeros((8, 128), jnp.float32),) * 4, unroll=unroll)
        for r in range(4):
            row_buf[it, b, r] = totals[r]
        if it == 0:
            pl.semaphore_wait(barrier, 37)
        for d in (1, 2, 3):
            mine = row_buf.at[it, b]
            remote(mine, mine, row_send.at[it], row_recv.at[it], (w, 4 * a + lax.rem(b + d, 4))).start()
        took(row_buf.at[it, pl.ds(0, 3)], row_recv.at[it])
        row_total = (row_buf[it, 0] + row_buf[it, 1]) + (row_buf[it, 2] + row_buf[it, 3])
        mass = worker_mass[pl.ds(pl.multiple_of(32 * a, 32), 32), :].reshape(4, 8, 128)
        worker_scale[it] = mass / row_total
        if it == ITERS - 1:
            out_buf[a] = SOFTMAX_TEMP * jnp.log(worker_scale[it])
            for d in (1, 2, 3):
                remote(out_buf.at[a], out_buf.at[a], out_send, out_recv, (w, lax.rem(z + 4 * d, 16))).start()

        def col_step(t, _):
            scale = in_line(worker_scale[it, lists[0, t]], range(8))
            sums = jnp.dot(in_two(scale), tiles[t], preferred_element_type=jnp.float32)
            part[t] = sums[0:1] + sums[1:2]
            return 0

        lax.fori_loop(0, slots, col_step, 0, unroll=unroll)
        sums = part[...].reshape(slots, RE)
        totals = jnp.dot(
            jnp.where(spot == spots[0:1, :slots], 1.0, 0.0), sums[:, :128],
            precision=lax.Precision.HIGHEST, preferred_element_type=jnp.float32,
        ) + jnp.dot(
            jnp.where(spot == spots[0:1, :slots] + 1, 1.0, 0.0), sums[:, 128:],
            precision=lax.Precision.HIGHEST, preferred_element_type=jnp.float32,
        )
        col_own[it] = totals.reshape(32, 8, 128)

        def scatter(d, _):
            to = lax.rem(w + d, 32)
            remote(col_own.at[it, to], col_buf.at[it, d - 1], col_send.at[it], col_recv.at[it], (to, z)).start()
            return 0

        lax.fori_loop(1, 32, scatter, 0)
        took(col_buf.at[it], col_recv.at[it])
        plane_buf[it, a] = col_own[it, w] + jnp.sum(col_buf[it], axis=0)
        for d in (1, 2, 3):
            mine = plane_buf.at[it, a]
            remote(mine, mine, plane_send.at[it], plane_recv.at[it], (w, lax.rem(z + 4 * d, 16))).start()
        took(plane_buf.at[it, pl.ds(0, 3)], plane_recv.at[it])
        column_total = (plane_buf[it, 0] + plane_buf[it, 1]) + (plane_buf[it, 2] + plane_buf[it, 3])
        scale_buf[it, w] = employer_mass[...] / column_total

        def share(d, _):
            mine = scale_buf.at[it, w]
            remote(mine, mine, scale_send.at[it], scale_recv.at[it], (lax.rem(w + d, 32), z)).start()
            return 0

        lax.fori_loop(1, 32, share, 0)
        took(scale_buf.at[it, pl.ds(0, 31)], scale_recv.at[it])

    for k in range(32):
        employer_out[2 * k : 2 * k + 2, :] = SOFTMAX_TEMP * jnp.log(scale_buf[ITERS - 1, k, pl.ds(2 * a, 2), :])
    took(out_buf.at[pl.ds(0, 3)], out_recv)
    worker_out[...] = out_buf[...].reshape(128, 128)

    took(out_buf.at[pl.ds(0, 3)], out_send)
    for it in range(ITERS):
        took(row_buf.at[it, pl.ds(0, 3)], row_send.at[it])
        took(col_buf.at[it], col_send.at[it])
        took(plane_buf.at[it, pl.ds(0, 3)], plane_send.at[it])
        took(scale_buf.at[it, pl.ds(0, 31)], scale_send.at[it])


def iterate(slots, cid, lists, rows, cols, spots, worker_mass, employer_mass):
    f32 = jnp.float32
    return pl.pallas_call(
        functools.partial(iterate_kernel, slots),
        out_shape=[jax.ShapeDtypeStruct((128, 128), f32), jax.ShapeDtypeStruct((64, 128), f32)],
        in_specs=[SMEM] + [VMEM] * 5,
        out_specs=[VMEM, VMEM],
        scratch_shapes=[
            pltpu.VMEM((slots, RW, RE), jnp.bfloat16),
            pltpu.VMEM((ITERS, 4, 4, 8, 128), f32),
            pltpu.VMEM((ITERS, 4, 8, 128), f32),
            pltpu.VMEM((slots, 1, RE), f32),
            pltpu.VMEM((ITERS, 32, 8, 128), f32),
            pltpu.VMEM((ITERS, 31, 8, 128), f32),
            pltpu.VMEM((ITERS, 4, 8, 128), f32),
            pltpu.VMEM((ITERS, 32, 8, 128), f32),
            pltpu.VMEM((4, 4, 8, 128), f32),
        ]
        + [DMA((ITERS,))] * 8
        + [DMA, DMA],
        compiler_params=pltpu.CompilerParams(
            collective_id=cid, has_side_effects=True, vmem_limit_bytes=(20 + slots // 2) << 20
        ),
        name=f"iterate_{slots}",
    )(lists, rows, cols, spots, worker_mass, employer_mass)


def shards(worker_emb, employer_emb, eligible, worker_mass, employer_mass):
    inputs = worker_emb, employer_emb, eligible, employer_mass.reshape(64, 128)
    inputs = [pltpu.with_memory_space_constraint(one, pltpu.HBM) for one in inputs]
    rows, cols, lists, spots, masses, peak = gather(*inputs)
    worker_mass = worker_mass.reshape(128, 128)

    def run(slots, cid):
        return lambda: iterate(slots, cid, lists, rows, cols, spots, worker_mass, masses)

    which = sum((peak[0, 0] > slots).astype(jnp.int32) for slots in SLOTS[:-1])
    worker_pot, employer_pot = lax.switch(which, [run(slots, k + 1) for k, slots in enumerate(SLOTS)])
    return worker_pot.reshape(-1), employer_pot.reshape(-1)


def solution(mesh):
    return jax.shard_map(
        shards,
        mesh=mesh,
        in_specs=(P(("wrk", "emp"), None), P("wrk", "emp"), P("wrk", "emp"), P("wrk"), P("emp")),
        out_specs=(P("wrk"), P("emp")),
        check_vma=False,
    )
```

time: 1140 us -> 165 us (0.14)
  waiting for transfers between devices: 527 us -> 0 us
  blocking collectives: 389 us -> 0 us
  Pallas kernels: 0 us -> 161 us
  matrix products: 144 us -> 0 us
  local copies, waits for them, and re-layouts: 29.9 us -> 1.76 us
  loops' own time: 17.5 us -> 0.24 us
  other arithmetic: 16 us -> 0 us
  between operations: 14.1 us -> 1.95 us
    psum x3 -> x0, blocking collectives: 389 us -> none  [shards(): column_total = lax.psum(col_local, 'wrk')]
    psum x3 -> x0, waiting for transfers between devices: 357 us -> none  [shards(): row_total = lax.psum(row_local, 'emp')]
    all_gather x2 -> x0, waiting for transfers between devices: 168 us -> none  [the longest x1 104 us: shards(): worker_rows = lax.all_gather(worker_emb, 'emp', axis=0, tiled=True)]
    pallas_call x0 -> x2, Pallas kernels: none -> 161 us  [the longest x1 82.8 us: iterate(): pl.pallas_call(functools.partial(iterate_kernel, slots), out_shape=[jax.S...]
    dot_general x96 -> x0, matrix products: 144 us -> none  [the longest x36 55.8 us: row_product(): jnp.dot(fetch(packed).astype(jnp.float32), packed[-1], precision=highest)]
    dynamic_slice x60 -> x0, local copies, waits for them, and re-layouts: 22.1 us -> none  [the longest x36 21 us: shards(): lax.map(lambda packed: make_tile(packed[0], packed[1], packed[2]), (row_i...]
    another operation x7 -> x1, loops' own time: 17.5 us -> 0.24 us  [shards(): lax.switch(which, [run(slots, k + 1) for k, slots in enumerate(SLOTS)])]
  transfers between devices with their start and end apart: 5 -> 0, of which waited for: 5 -> 0; matrix products, arithmetic and copies ran while one was open for 1% -> 0% of each run, Pallas kernels for 0% -> 0%
where the time goes in v2:
time: 165 us
  Pallas kernels  161 us (98%)
  between operations  1.95 us (1%)
  local copies, waits for them, and re-layouts  1.76 us (1%)
    pallas_call x1, Pallas kernels, iterate(): pl.pallas_call(functools.partial(iterate_kernel, slots), out_shape=[jax.S...  82.8 us
    pallas_call x1, Pallas kernels, gather(): pl.pallas_call(gather_kernel, out_shape=[jax.ShapeDtypeStruct((4, RW, E),...  78 us

profile of v2, /device:TPU:1, one launch (start us, length us, event | category | flops | bytes accessed | tf_op | source)
XLA Modules:
  0.0 164.8 jit_solution(6653475748502885671)
XLA Ops:
  0.6 78.0 %gather.1 = (bf16[4,1024,256]{2,1,0:T(8,128)(2,1)S(1)}, bf16[4,2,4,4,2,2,4,16,256]{8,7,6,5,4,3,2,1,0:T(8,128)(2,1)S(1)}, s32[8,128]{1,0:T(8,128)S(1)}, s32[8,128...) custom-call(bf16[1024,256]{1,0:T(8,128)(2,1)} %wk.1, bf16[8,8192]{1,0:T(8,128)(2,1)} %em_all.1, ...), custom_call_target="tpu_custom_call" | custom-call | tf_op jit(solution)/shard_map/gather/pallas_call | solution.py:328
  78.7 0.5 slice.4
  80.5 83.0 %conditional.1 = ((f32[128,128]{1,0:T(8,128)S(1)}, f32[64,128]{1,0:T(8,128)S(1)})) conditional(s32[]{:T(128)} %bitcast.1, (s32[8,128]{1,0:T(8,128)S(1)}, bf16[4,1024,256]{2,1,0:T(8,128)(2,1)S(1)}, bf16[4,2,4,4,2,2,4,16,256]{8,7,6,5,4,3,2,1,0:T(8,128)(2,1)S(1)}, s32[8,128]{1,0:T(8,128)S(1)}, f32[128,128]{1,0:T(8,128)}, ...), branch_computations={%region_0.0_spmd, %region_1.0_spmd, %region_2.0_spmd} | conditional | bytes 8 | solution.py:548
  80.5 82.8 %iterate_13.1 = (f32[128,128]{1,0:T(8,128)S(1)}, f32[64,128]{1,0:T(8,128)S(1)}) custom-call(s32[8,128]{1,0:T(8,128)S(1)} %get-tuple-element.44.lists, bf16[4,1024,256]{2,1,0:T(8,128)(2,1)S(1)} %get-tuple-element.45.rows, bf16[4,2,4,4,2,2,4,16,256]{8,7,6,5,4,3,2,1,0:T(8,128)(2,1)S(1)} %get-tuple-element.46.cols, s32[8,128]{1,0:T(8,128)S(1)} %get-tuple-element.47.spots, ...), custom_call_target="tpu_custom_call" | custom-call | tf_op jit(solution)/shard_map/cond/branch_0_fun/iterate_13/pallas_call | solution.py:513
  163.5 0.6 copy.15
  164.2 0.6 copy.16

commit v3 on v2

--- a/solution.py
+++ b/solution.py
@@ -17,13 +17,13 @@
 CHUNKS = 4
 ORDER = (
     "Z", "o0", "o1", "f00", "f01", "f02", "f03", "f10", "f11", "f12", "f13", "s00", "s01", "R", "s10", "s11",
-    "o2", "o3", "t00", "t01", "t02", "t03", "t10", "t11", "t12", "t13", "f20", "f21", "f22", "f23", "f30", "o4",
-    "o5", "f31", "f32", "f33", "r10", "e0", "s21", "s20", "e1", "r11", "f40", "f41", "f42", "f43", "f51", "s30",
-    "s31", "f50", "f52", "f53", "r12", "t20", "t21", "t22", "t23", "s40", "s41", "r13", "t30", "t31", "t32",
-    "t33", "s50", "s51", "e2", "t40", "t41", "t42", "t43", "o6", "o7", "m0", "r20", "e3", "t50", "t51", "t52",
-    "t53", "r21", "m1", "e4", "f60", "f61", "f62", "f63", "f70", "f71", "f72", "f73", "r22", "e5", "s60", "s61",
-    "m2", "s70", "s71", "r23", "m3", "r30", "t60", "t61", "t62", "t63", "r31", "m4", "t70", "t71", "t72", "t73",
-    "e6", "r32", "m5", "e7", "r33", "m6", "m7",
+    "n", "o2", "o3", "t00", "t01", "t02", "t03", "t10", "t11", "t12", "t13", "f20", "f21", "f22", "f23", "f30",
+    "o4", "o5", "f31", "f32", "f33", "r10", "e0", "s21", "s20", "e1", "r11", "f40", "f41", "f42", "f43", "f51",
+    "s30", "s31", "f50", "f52", "f53", "r12", "t20", "t21", "t22", "t23", "s40", "s41", "r13", "m0", "t30",
+    "t31", "t32", "t33", "s50", "s51", "e2", "t40", "t41", "t42", "t43", "o6", "o7", "e3", "m1", "r20", "t50",
+    "t51", "t52", "t53", "r21", "e4", "f60", "f61", "f62", "f63", "f70", "f71", "f72", "f73", "r22", "m2",
+    "s60", "s61", "e5", "s70", "s71", "r23", "r30", "t60", "t61", "t62", "t63", "m3", "r31", "t70", "t71",
+    "t72", "t73", "e6", "r32", "e7", "r33",
 )
 MESH = pl.DeviceIdType.MESH
 VMEM = pl.BlockSpec(memory_space=pltpu.VMEM)
@@ -53,7 +53,7 @@
 
 def gather_kernel(
     wk, em_all, eligible_all, mass_all,
-    rows, cols, lists, spots, masses, peak,
+    rows, cols, lists, spots, masses, which,
     em, eligible, mass, shard, small_all, top, top_all,
     load_sem, keep_sem, z_send, z_recv, xy_send, xy_recv, core_send, core_recv,
     row_send, row_recv, small_send, small_recv, top_send, top_recv,
@@ -71,10 +71,10 @@
     ]
     for one in loads:
         one.start()
-    top_all[...] = jnp.zeros_like(top_all)
     barrier = pltpu.get_barrier_semaphore()
-    beside = [(w, 4 * a + lax.rem(b + d, 4)) for d in (1, 3)]
-    for to in (left, right, down, up, back, ahead, twin, *beside):
+    group = [(w, 4 * a + lax.rem(b + d, 4)) for d in (1, 2, 3)]
+    far = [device(x + 2, y, c, z), device(x, y + 2, c, z)]
+    for to in (left, right, down, up, back, ahead, twin, *group, *far):
         pl.semaphore_signal(barrier, inc=1, device_id=to, device_id_type=MESH)
 
     for one in loads:
@@ -96,7 +96,7 @@
     ]
     for one in keep:
         one.start()
-    pl.semaphore_wait(barrier, 9)
+    pl.semaphore_wait(barrier, 12)
 
     xs = [lax.rem(x + i, 4) for i in range(4)]
     ys = [lax.rem(y + i, 4) for i in range(4)]
@@ -113,12 +113,16 @@
         return ref.at[pl.ds(2 * k, 2)] if len(ref.shape) == 3 else ref.at[:, pl.ds(2 * k, 2)]
 
     def z_own():
+        for g, to in enumerate((ahead, back)):
+            remote(small_all.at[a], small_all.at[a], small_send, small_recv.at[g], to).start()
         for k in range(2):
             for g, to in enumerate((ahead, back)):
                 remote(shard.at[k], cols.at[a, k, x, y, c], z_send, z_recv.at[g, k], to).start()
-            if k == 0:
-                for g, to in enumerate((ahead, back)):
-                    remote(small_all.at[a], small_all.at[a], small_send, small_recv.at[g], to).start()
+
+    def relay_small():
+        few = small_all.at[ps[3]]
+        took(few, small_recv.at[0])
+        remote(few, few, small_send, small_recv.at[2], ahead).start()
 
     def own(s):
         got = part(s).at[x, y, c]
@@ -127,10 +131,6 @@
             took(got, z_recv.at[g, k])
             if g == k:
                 remote(got, got, z_send, z_recv.at[2, k], (ahead, back)[g]).start()
-            if s == 2:
-                few = small_all.at[ps[3]]
-                took(few, small_recv.at[0])
-                remote(few, few, small_send, small_recv.at[2], ahead).start()
         if s >= 6:
             took(got, z_recv.at[2, s - 6])
         for k in range(4):
@@ -145,22 +145,26 @@
         took(got, xy_recv.at[s, k])
         push(lanes(got, k % 2), k, 1, xy_recv.at[s, 4 + k // 2])
 
+    def to_twin(line):
+        remote(line, line, core_send, core_recv, twin).start()
+
     def second(s, axis):
         took(part(s).at[x, y, c, axis], xy_recv.at[s, 4 + axis])
         line = part(s).at[:, y, c, 0] if axis == 0 else part(s).at[x, :, c, 1]
         for k in range(2):
             push(line, 2 - 2 * axis + k, 2, xy_recv.at[s, 6 + 2 * axis + k])
+        to_twin(line)
 
     def third(s, k):
         line = part(s).at[:, ys[3 - 2 * k], c, 0] if k < 2 else part(s).at[xs[7 - 2 * k], :, c, 1]
         took(line, xy_recv.at[s, 6 + k])
         push(lanes(line, k % 2), (2, 3, 0, 1)[k], 3, xy_recv.at[s, 10 + k // 2])
+        to_twin(line)
 
     def finish(s):
-        took(part(s).at[:, y, c, 0], xy_recv.at[s, 10])
-        took(part(s).at[:, y, c, 0], xy_recv.at[s, 11])
-        got = part(s).at[:, :, c]
-        remote(got, got, core_send, core_recv, twin).start()
+        for k, line in enumerate((part(s).at[:, ys[2], c, 0], part(s).at[xs[2], :, c, 1])):
+            took(line, xy_recv.at[s, 10 + k])
+            to_twin(line)
 
     def row_chunk(block, j):
         return block.at[pl.ds(j * (RW // CHUNKS), RW // CHUNKS)]
@@ -241,52 +245,33 @@
         lists[...] = table
         spots[...] = jnp.broadcast_to(col * 8 + plane * 2, (8, 128))
 
-    def top_send_to(k, g, to):
-        remote(top.at[k], top_all.at[k, g], top_send.at[k, g], top_recv.at[k, g], to).start()
+    circles = (
+        [device(x + d, y, c, z) for d in (1, 2, 3)],
+        [device(x, y + d, c, z) for d in (1, 2, 3)],
+        group,
+        [twin],
+    )
 
     def maximum(k):
         if k == 0:
             list_tiles()
         else:
-            if k <= 4:
-                for g in range(2):
-                    took(top_all.at[k - 1, g], top_recv.at[k - 1, g])
-            else:
-
-                @pl.when(b > 0)
-                def _():
-                    took(top_all.at[k - 1, 0], top_recv.at[k - 1, 0])
-
-                @pl.when(b < 3)
-                def _():
-                    took(top_all.at[k - 1, 1], top_recv.at[k - 1, 1])
-
-            top[k] = jnp.maximum(top[k - 1], jnp.maximum(top_all[k - 1, 0], top_all[k - 1, 1]))
-        if k < 4:
-            for g in range(2):
-                top_send_to(k, g, near[2 * (k // 2) + g])
-        elif k < 7:
-
-            @pl.when(b < 3)
-            def _():
-                top_send_to(k, 0, (w, z + 1))
-
-            @pl.when(b > 0)
-            def _():
-                top_send_to(k, 1, (w, z - 1))
-
-        else:
-            top_send_to(k, 0, twin)
+            for d in range(3):
+                took(top_all.at[k - 1, d], top_recv.at[k - 1, d])
+            top[k] = jnp.maximum(top[k - 1], jnp.max(top_all[k - 1], axis=0))
+        for d, to in enumerate(circles[k]):
+            remote(top.at[k], top_all.at[k, d], top_send.at[k, d], top_recv.at[k, d], to).start()
 
     steps = dict(
-        m=maximum,
+        m=maximum, n=relay_small,
         Z=z_own, o=own, f=first, s=second, t=third, e=finish, R=send_rows, r=relay,
     )
     for step in ORDER:
         steps[step[0]](*map(int, step[1:]))
 
-    took(top_all.at[7, 0], top_recv.at[7, 0])
-    peak[...] = jnp.maximum(top[7], top_all[7, 0])
+    took(top_all.at[3, 0], top_recv.at[3, 0])
+    most = jnp.max(jnp.maximum(top[3], top_all[3, 0]))
+    which[0, 0] = sum(jnp.where(most > slots, 1, 0) for slots in SLOTS[:-1]).astype(jnp.int32)
 
     keep[1].wait()
     took(cols.at[pl.ds(0, 2)], core_recv)
@@ -299,18 +284,8 @@
     took(cols.at[0, 0, 0, pl.ds(0, 3)], z_send)
     took(small_all.at[pl.ds(0, 3)], small_send)
     for k in range(4):
-        for g in range(2):
-            took(top.at[k], top_send.at[k, g])
-    took(top.at[7], top_send.at[7, 0])
-    for k in range(4, 7):
-
-        @pl.when(b < 3)
-        def _():
-            took(top.at[k], top_send.at[k, 0])
-
-        @pl.when(b > 0)
-        def _():
-            took(top.at[k], top_send.at[k, 1])
+        for d in range(len(circles[k])):
+            took(top.at[k], top_send.at[k, d])
 
     for d in range(3):
 
@@ -333,20 +308,20 @@
             jax.ShapeDtypeStruct((8, 128), jnp.int32),
             jax.ShapeDtypeStruct((8, 128), jnp.int32),
             jax.ShapeDtypeStruct((8, 128), f32),
-            jax.ShapeDtypeStruct((8, 128), f32),
+            jax.ShapeDtypeStruct((1, 1), jnp.int32),
         ],
         in_specs=[HBM] * 4,
-        out_specs=[VMEM] * 6,
+        out_specs=[VMEM] * 5 + [SMEM],
         scratch_shapes=[
             pltpu.VMEM((8, 8192), jnp.bfloat16),
             pltpu.VMEM((16, 32), jnp.int32),
             pltpu.VMEM((64, 128), f32),
             pltpu.VMEM((2, 2, 4, 16, RE), jnp.bfloat16),
             pltpu.VMEM((4, 24, 128), f32),
-            pltpu.VMEM((8, 8, 128), f32),
-            pltpu.VMEM((8, 2, 8, 128), f32),
+            pltpu.VMEM((4, 8, 128), f32),
+            pltpu.VMEM((4, 3, 8, 128), f32),
             DMA((3,)), DMA((2,)), DMA, DMA((3, 2)), DMA((4, 4)), DMA((8, 12)), DMA, DMA,
-            DMA((2, 3)), DMA((2, 3, CHUNKS)), DMA, DMA((3,)), DMA((8, 2)), DMA((8, 2)),
+            DMA((2, 3)), DMA((2, 3, CHUNKS)), DMA, DMA((3,)), DMA((4, 3)), DMA((4, 3)),
         ],
         compiler_params=pltpu.CompilerParams(collective_id=0, has_side_effects=True, vmem_limit_bytes=24 << 20),
         name="gather",
@@ -538,14 +513,13 @@
 def shards(worker_emb, employer_emb, eligible, worker_mass, employer_mass):
     inputs = worker_emb, employer_emb, eligible, employer_mass.reshape(64, 128)
     inputs = [pltpu.with_memory_space_constraint(one, pltpu.HBM) for one in inputs]
-    rows, cols, lists, spots, masses, peak = gather(*inputs)
+    rows, cols, lists, spots, masses, which = gather(*inputs)
     worker_mass = worker_mass.reshape(128, 128)
 
     def run(slots, cid):
         return lambda: iterate(slots, cid, lists, rows, cols, spots, worker_mass, masses)
 
-    which = sum((peak[0, 0] > slots).astype(jnp.int32) for slots in SLOTS[:-1])
-    worker_pot, employer_pot = lax.switch(which, [run(slots, k + 1) for k, slots in enumerate(SLOTS)])
+    worker_pot, employer_pot = lax.switch(which[0, 0], [run(slots, k + 1) for k, slots in enumerate(SLOTS)])
     return worker_pot.reshape(-1), employer_pot.reshape(-1)
 
 

time: 165 us -> 163 us (0.988); the launches traced: 165 us -> 165 us
    pallas_call x1, Pallas kernels: 82.8 us -> 89.2 us  [iterate(): pl.pallas_call(functools.partial(iterate_kernel, slots), out_shape=[jax.S...]
    pallas_call x1, Pallas kernels: 78 us -> 72.9 us  [gather(): pl.pallas_call(gather_kernel, out_shape=[jax.ShapeDtypeStruct((4, RW, E),...]
where the time goes in v3:
time: 163 us; the launch traced here: 165 us
  Pallas kernels  162 us (99%)
    pallas_call x1, Pallas kernels, iterate(): pl.pallas_call(functools.partial(iterate_kernel, slots), out_shape=[jax.S...  89.2 us
    pallas_call x1, Pallas kernels, gather(): pl.pallas_call(gather_kernel, out_shape=[jax.ShapeDtypeStruct((4, RW, E),...  72.9 us

profile of v3, /device:TPU:1, one launch (start us, length us, event | category | flops | bytes accessed | tf_op | source)
XLA Modules:
  0.0 165.4 jit_solution(523660068939142882)
XLA Ops:
  0.6 72.9 %gather.1 = (bf16[4,1024,256]{2,1,0:T(8,128)(2,1)S(1)}, bf16[4,2,4,4,2,2,4,16,256]{8,7,6,5,4,3,2,1,0:T(8,128)(2,1)S(1)}, s32[8,128]{1,0:T(8,128)S(1)}, s32[8,128...) custom-call(bf16[1024,256]{1,0:T(8,128)(2,1)} %wk.1, bf16[8,8192]{1,0:T(8,128)(2,1)} %em_all.1, ...), custom_call_target="tpu_custom_call" | custom-call | tf_op jit(solution)/shard_map/gather/pallas_call | solution.py:303
  74.1 90.0 %conditional.1 = ((f32[128,128]{1,0:T(8,128)S(1)}, f32[64,128]{1,0:T(8,128)S(1)})) conditional(s32[]{:T(128)} %bitcast.1, (s32[8,128]{1,0:T(8,128)S(1)}, bf16[4,1024,256]{2,1,0:T(8,128)(2,1)S(1)}, bf16[4,2,4,4,2,2,4,16,256]{8,7,6,5,4,3,2,1,0:T(8,128)(2,1)S(1)}, s32[8,128]{1,0:T(8,128)S(1)}, f32[128,128]{1,0:T(8,128)}, ...), branch_computations={%region_0.0_spmd, %region_1.0_spmd, %region_2.0_spmd} | conditional | bytes 8 | solution.py:522
  74.4 89.2 %iterate_17.1 = (f32[128,128]{1,0:T(8,128)S(1)}, f32[64,128]{1,0:T(8,128)S(1)}) custom-call(s32[8,128]{1,0:T(8,128)S(1)} %get-tuple-element.52.lists, bf16[4,1024,256]{2,1,0:T(8,128)(2,1)S(1)} %get-tuple-element.53.rows, bf16[4,2,4,4,2,2,4,16,256]{8,7,6,5,4,3,2,1,0:T(8,128)(2,1)S(1)} %get-tuple-element.54.cols, s32[8,128]{1,0:T(8,128)S(1)} %get-tuple-element.55.spots, ...), custom_call_target="tpu_custom_call" | custom-call | tf_op jit(solution)/shard_map/cond/branch_1_fun/iterate_17/pallas_call | solution.py:488
  164.1 0.6 copy.15
  164.8 0.6 copy.16

commit v4 on v3

--- a/solution.py
+++ b/solution.py
@@ -365,6 +365,16 @@
     return jnp.where(at == 0, high, jnp.where(at == 1, wide - high, 0.0)).astype(jnp.bfloat16)
 
 
+def placed(matrix, values):
+    high = values.astype(jnp.bfloat16)
+    rest = values - high.astype(jnp.float32)
+    middle = rest.astype(jnp.bfloat16)
+    low = (rest - middle.astype(jnp.float32)).astype(jnp.bfloat16)
+    parts = jnp.concatenate([high, middle, low], axis=1)
+    out = jnp.dot(matrix, parts, preferred_element_type=jnp.float32)
+    return (out[:, :128] + out[:, 128:256]) + out[:, 256:]
+
+
 def iterate_kernel(
     slots,
     lists, rows, cols, spots, worker_mass, employer_mass,
@@ -393,6 +403,8 @@
     lax.fori_loop(0, slots, build_step, 0)
     unroll = slots if slots <= 20 else 4
     spot = lax.broadcasted_iota(jnp.int32, (256, slots), 0)
+    to_first = jnp.where(spot == spots[0:1, :slots], 1.0, 0.0).astype(jnp.bfloat16)
+    to_second = jnp.where(spot == spots[0:1, :slots] + 1, 1.0, 0.0).astype(jnp.bfloat16)
     block_line = lax.broadcasted_iota(jnp.int32, (8, 128), 0)
 
     for it in range(ITERS):
@@ -438,13 +450,7 @@
 
         lax.fori_loop(0, slots, col_step, 0, unroll=unroll)
         sums = part[...].reshape(slots, RE)
-        totals = jnp.dot(
-            jnp.where(spot == spots[0:1, :slots], 1.0, 0.0), sums[:, :128],
-            precision=lax.Precision.HIGHEST, preferred_element_type=jnp.float32,
-        ) + jnp.dot(
-            jnp.where(spot == spots[0:1, :slots] + 1, 1.0, 0.0), sums[:, 128:],
-            precision=lax.Precision.HIGHEST, preferred_element_type=jnp.float32,
-        )
+        totals = placed(to_first, sums[:, :128]) + placed(to_second, sums[:, 128:])
         col_own[it] = totals.reshape(32, 8, 128)
 
         def scatter(d, _):

time: 163 us -> 159 us (0.975); the launches traced: 165 us -> 159 us
  Pallas kernels: 162 us -> 156 us
    pallas_call x1, Pallas kernels: 89.2 us -> 83.5 us  [iterate(): pl.pallas_call(functools.partial(iterate_kernel, slots), out_shape=[jax.S...]
where the time goes in v4:
time: 159 us
  Pallas kernels  156 us (98%)
    pallas_call x1, Pallas kernels, iterate(): pl.pallas_call(functools.partial(iterate_kernel, slots), out_shape=[jax.S...  83.5 us
    pallas_call x1, Pallas kernels, gather(): pl.pallas_call(gather_kernel, out_shape=[jax.ShapeDtypeStruct((4, RW, E),...  72.9 us

profile of v4, /device:TPU:1, one launch (start us, length us, event | category | flops | bytes accessed | tf_op | source)
XLA Modules:
  0.0 159.1 jit_solution(12860881140836800602)
XLA Ops:
  0.6 72.9 %gather.1 = (bf16[4,1024,256]{2,1,0:T(8,128)(2,1)S(1)}, bf16[4,2,4,4,2,2,4,16,256]{8,7,6,5,4,3,2,1,0:T(8,128)(2,1)S(1)}, s32[8,128]{1,0:T(8,128)S(1)}, s32[8,128...) custom-call(bf16[1024,256]{1,0:T(8,128)(2,1)} %wk.1, bf16[8,8192]{1,0:T(8,128)(2,1)} %em_all.1, ...), custom_call_target="tpu_custom_call" | custom-call | tf_op jit(solution)/shard_map/gather/pallas_call | solution.py:303
  74.1 83.8 %conditional.1 = ((f32[128,128]{1,0:T(8,128)S(1)}, f32[64,128]{1,0:T(8,128)S(1)})) conditional(s32[]{:T(128)} %bitcast.1, (s32[8,128]{1,0:T(8,128)S(1)}, bf16[4,1024,256]{2,1,0:T(8,128)(2,1)S(1)}, bf16[4,2,4,4,2,2,4,16,256]{8,7,6,5,4,3,2,1,0:T(8,128)(2,1)S(1)}, s32[8,128]{1,0:T(8,128)S(1)}, f32[128,128]{1,0:T(8,128)}, ...), branch_computations={%region_0.0_spmd, %region_1.0_spmd, %region_2.0_spmd} | conditional | bytes 8 | solution.py:528
  74.1 83.5 %iterate_13.1 = (f32[128,128]{1,0:T(8,128)S(1)}, f32[64,128]{1,0:T(8,128)S(1)}) custom-call(s32[8,128]{1,0:T(8,128)S(1)} %get-tuple-element.44.lists, bf16[4,1024,256]{2,1,0:T(8,128)(2,1)S(1)} %get-tuple-element.45.rows, bf16[4,2,4,4,2,2,4,16,256]{8,7,6,5,4,3,2,1,0:T(8,128)(2,1)S(1)} %get-tuple-element.46.cols, s32[8,128]{1,0:T(8,128)S(1)} %get-tuple-element.47.spots, ...), custom_call_target="tpu_custom_call" | custom-call | tf_op jit(solution)/shard_map/cond/branch_0_fun/iterate_13/pallas_call | solution.py:494
  157.9 0.6 copy.15
  158.5 0.6 copy.16
